TPU v7x, 32 devices: a whole 2x2x4 slice. The times are simulated.
32 devices in a mesh: cache: 4 (over z), head: 8 (over y, x, core).
Axes of the slice: x: 2, y: 2, z: 4, core: 2. Of those that a mesh axis runs over, the one named last changes fastest.
Arguments:
- delta_query: bfloat16 [16, 512, 2048], P('cache', None, 'head'), may hold values from -6 to 6
- delta_key: bfloat16 [16, 512, 2048], P('cache', None, 'head'), may hold values from -6 to 6
- delta_value: bfloat16 [16, 512, 4096], P('cache', None, 'head'), may hold values from -6 to 6
- delta_gate: bfloat16 [16, 512, 4096], P('cache', None, 'head'), may hold values from -6 to 6
- write_strength: float32 [16, 32, 512], P('cache', 'head'), may hold values from 0.1 to 0.95
- decay_log: float32 [16, 32, 512], P('cache', 'head'), may hold values from -1.5 to 0
- kept_state: float32 [16, 32, 128, 128], P('cache', 'head'), may hold values from -6 to 6
- kept_kv: bfloat16 [16, 1024, 2, 512], P('cache', 'head'), may hold values from -8 to 8
- fresh_kv: bfloat16 [16, 512, 2, 512], P('cache', 'head'), may hold values from -6 to 6
- attn_query: bfloat16 [16, 512, 4096], P('cache', None, 'head'), may hold values from -100 to 100
- attn_gate: bfloat16 [16, 512, 4096], P('cache', None, 'head'), may hold values from -6 to 6
- cached_len: int32 [16], replicated, may hold values from 2 to 1024, as said below
- slot_of_session: int32 [16], replicated, may hold values from 0 to 15, as said below
- delta_out_weight: bfloat16 [4096, 2048], P('head'), may hold values from -0.09375 to 0.09375
- attn_out_weight: bfloat16 [4096, 2048], P('head'), may hold values from -0.75 to 0.75
Outputs:
- delta_mixed: bfloat16 [8192, 2048], P(('cache', 'head'))
- attn_mixed: bfloat16 [8192, 2048], P(('cache', 'head'))
- final_state: float32 [16, 32, 128, 128], P('cache', 'head')
Inputs may be any that keep to these rules, and one draw needn't show every extreme that they name: `slot_of_session`: a permutation of the slots; slot r lies on cache shard floor(r / 4); session s belongs to owner floor(s / 4), and the 4 sessions of one owner are kept on 4 different shards. `cached_len`: some session keeps exactly 1024 positions.
All inputs are finite; a program needn't handle non-finite values.
Results may differ from a plain program's by a relative error of at most 0.02.
Values may be sent and summed in bfloat16 or wider, within the bound.
A program may use at most 128 MiB of HBM per device.

v0:
```python
import functools
import math

import jax
import jax.numpy as jnp
from jax import lax
from jax.experimental import pallas as pl
from jax.experimental.pallas import tpu as pltpu
from jax.sharding import PartitionSpec as P

LK = 128
LV = 128
AH = 16
KVH = 2
HD = 256
BLOCK = 128
PAIR = 2
CHUNKS = 2

big_negative = -1e30
f32 = jnp.float32
bf16 = jnp.bfloat16


def mm(a, b, dims=((1,), (0,))):
    return lax.dot_general(a, b, (dims, ((), ())), preferred_element_type=f32)


def delta_kernel(source, q_ref, k_ref, v_ref, gate_ref, row_ref, col_ref, start_ref, heads_ref, state_ref):
    pair = pl.program_id(0)
    sessions, _, q_cols = q_ref.shape
    key_heads = q_cols // LK
    value_heads = v_ref.shape[2] // LV
    ratio = value_heads // key_heads

    @pl.when(pl.program_id(1) == 0)
    def _():
        for s in range(sessions):
            state_ref[s] = start_ref[source[pair * sessions + s]].astype(f32)

    rows = lax.broadcasted_iota(jnp.int32, (BLOCK, BLOCK), 0)
    cols = lax.broadcasted_iota(jnp.int32, (BLOCK, BLOCK), 1)
    inclusive = rows >= cols
    differ = jnp.where(rows > cols, rows ^ cols, 0)
    eye = jnp.where(rows == cols, 1.0, 0.0).astype(f32)

    work = []
    for s in range(sessions):
        for a in range(key_heads):
            span = slice(a * LK, (a + 1) * LK)
            q = q_ref[s, :, span].astype(f32)
            k = k_ref[s, :, span].astype(f32)
            q = q * (lax.rsqrt(jnp.sum(q * q, axis=-1, keepdims=True) + 1e-06) * (1.0 / math.sqrt(LK)))
            k = k * lax.rsqrt(jnp.sum(k * k, axis=-1, keepdims=True) + 1e-06)
            qb, kb = q.astype(bf16), k.astype(bf16)
            key_key = mm(kb, kb, ((1,), (1,)))
            query_key = mm(qb, kb, ((1,), (1,)))
            for j in range(a * ratio, (a + 1) * ratio):
                run_row = row_ref[s, j : j + 1, :]
                run_col = col_ref[s, :, j : j + 1]
                strength = col_ref[s, :, value_heads + j : value_heads + j + 1]
                fall = jnp.where(inclusive, jnp.exp(jnp.minimum(run_col - run_row, 0.0)), 0.0)
                lower = strength * fall * key_key
                mixed = (fall * query_key).astype(bf16)
                growth = jnp.exp(run_col)
                v = v_ref[s, :, j * LV : (j + 1) * LV].astype(f32)
                right = jnp.concatenate([(strength * growth) * k, strength * v], axis=1).astype(bf16)
                last = run_row[:, BLOCK - 1 : BLOCK]
                tail = (jnp.exp(last - run_col) * k).astype(bf16)
                work.append((s, j, lower, mixed, (growth * q).astype(bf16), right, tail, jnp.exp(last)))

    inverses = [eye - jnp.where(differ == 1, item[2], 0.0) for item in work]
    for level in range(1, BLOCK.bit_length() - 1):
        mask = (differ >> level) == 1
        small = [t.astype(bf16) for t in inverses]
        first = [
            mm(jnp.where(mask, item[2], 0.0).astype(bf16), t).astype(bf16) for item, t in zip(work, small)
        ]
        inverses = [t - mm(b, x) for t, b, x in zip(inverses, small, first)]

    solved = [mm(t.astype(bf16), item[5]) for t, item in zip(inverses, work)]
    for item, x in zip(work, solved):
        s, j, _, mixed, q_grown, _, tail, fade = item
        state = state_ref[s, j]
        seen = mm(jnp.concatenate([x[:, :LK].astype(bf16), q_grown], axis=0), state.astype(bf16))
        update = (x[:, LK:] - seen[:BLOCK]).astype(bf16)
        state_ref[s, j] = fade * state + mm(tail, update, ((0,), (0,)))
        emitted = seen[BLOCK:] + mm(mixed, update)
        scale = lax.rsqrt(jnp.mean(emitted * emitted, axis=-1, keepdims=True) + 1e-06)
        gate = gate_ref[s, :, j * LV : (j + 1) * LV].astype(f32)
        heads_ref[s, :, j * LV : (j + 1) * LV] = (emitted * scale * (gate / (1.0 + jnp.exp(-gate)))).astype(bf16)


def delta_layer(q, k, v, gate, strength, decay, start, source):
    count, fresh_len, value_cols = v.shape
    value_heads = value_cols // LV
    running = jnp.cumsum(decay.reshape(count, value_heads, fresh_len // BLOCK, BLOCK), axis=-1)
    running = running.reshape(count, value_heads, fresh_len)
    columns = jnp.concatenate([running, strength], axis=1).transpose(0, 2, 1)

    def rows(width):
        return pl.BlockSpec((PAIR, BLOCK, width), lambda s, c, _: (s, c, 0))

    return pl.pallas_call(
        delta_kernel,
        grid_spec=pltpu.PrefetchScalarGridSpec(
            num_scalar_prefetch=1,
            grid=(count // PAIR, fresh_len // BLOCK),
            in_specs=[
                rows(q.shape[2]),
                rows(k.shape[2]),
                rows(value_cols),
                rows(value_cols),
                pl.BlockSpec((PAIR, value_heads, BLOCK), lambda s, c, _: (s, 0, c)),
                rows(2 * value_heads),
                pl.BlockSpec(start.shape, lambda s, c, _: (0, 0, 0, 0)),
            ],
            out_specs=[
                rows(value_cols),
                pl.BlockSpec((PAIR, value_heads, LK, LV), lambda s, c, _: (s, 0, 0, 0)),
            ],
        ),
        out_shape=[
            jax.ShapeDtypeStruct((count, fresh_len, value_cols), bf16),
            jax.ShapeDtypeStruct((count, value_heads, LK, LV), f32),
        ],
        compiler_params=pltpu.CompilerParams(vmem_limit_bytes=40 * 2**20),
        cost_estimate=pl.CostEstimate(flops=4 * 10**10, bytes_accessed=12 * 10**6, transcendentals=0),
        name="delta_layer",
    )(source, q, k, v, gate, running, columns, start)


def attend_kernel(chunk, block_rows, devices, scalars, lengths, q_ref, gate_ref, near_ref, far_ref, fresh_ref, out_ref):
    s = pl.program_id(0)
    me = scalars[1]
    length = lengths[s]
    _, blocks, part, width = q_ref.shape
    rows = blocks * part
    heads = width // HD
    slots, _, _, kept_rows, _ = near_ref.shape
    kept = slots * kept_rows
    bits = devices.bit_length() - 1

    def penalty(far):
        lane = lax.broadcasted_iota(jnp.int32, (1, kept), 1)
        slot = lane // kept_rows + far * slots
        code = jnp.zeros_like(slot)
        for i in range(bits):
            code = code + ((slot >> i) & 1) * (1 << (bits - 1 - i))
        place = (code ^ me) * kept_rows + lane % kept_rows
        return jnp.where(place < length, 0.0, big_negative).astype(f32)

    fresh = fresh_ref.shape[0] * fresh_ref.shape[3]
    row = lax.broadcasted_iota(jnp.int32, (rows, fresh), 0)
    now = (row // part) * block_rows + chunk * part + row % part
    causal = lax.broadcasted_iota(jnp.int32, (rows, fresh), 1) <= now
    near_off, far_off = penalty(0), penalty(1)

    keys = [
        near_ref[:, 0, 0].reshape(kept, HD),
        far_ref[:, 0, 0].reshape(kept, HD),
        fresh_ref[:, 0, 0].reshape(fresh, HD),
    ]
    values = [
        near_ref[:, 0, 1].reshape(kept, HD),
        far_ref[:, 0, 1].reshape(kept, HD),
        fresh_ref[:, 1, 0].reshape(fresh, HD),
    ]
    for h in range(heads):
        q = q_ref[0, :, :, h * HD : (h + 1) * HD].reshape(rows, HD)
        near = mm(q, keys[0], ((1,), (1,))) + near_off
        far = mm(q, keys[1], ((1,), (1,))) + far_off
        new = jnp.where(causal, mm(q, keys[2], ((1,), (1,))), big_negative)
        peak = jnp.max(jnp.maximum(jnp.maximum(near, far), new) if kept == fresh else new, axis=-1, keepdims=True)
        if kept != fresh:
            peak = jnp.maximum(peak, jnp.max(jnp.maximum(near, far), axis=-1, keepdims=True))
        weights = [jnp.exp((x - peak) * (1.0 / math.sqrt(HD))) for x in (near, far, new)]
        total = sum(jnp.sum(w, axis=-1, keepdims=True) for w in weights)
        mixed = sum(mm(w.astype(bf16), v) for w, v in zip(weights, values))
        gate = gate_ref[0, :, :, h * HD : (h + 1) * HD].reshape(rows, HD).astype(f32)
        gated = mixed / (total * (1.0 + jnp.exp(-gate)))
        out_ref[0, :, :, h * HD : (h + 1) * HD] = gated.astype(bf16).reshape(blocks, part, HD)


def attend(chunk, block_rows, devices, q, gate, near, far, fresh, scalars, lengths, source):
    count, blocks, _, width = q.shape
    part = block_rows // CHUNKS
    scalars = jnp.concatenate([scalars, source])
    slots, _, _, kept_rows, _ = near.shape
    rows = pl.BlockSpec((1, blocks, part, width), lambda s, m, n: (s, 0, chunk, 0))
    kept = pl.BlockSpec((slots, 1, 2, kept_rows, HD), lambda s, m, n: (0, m[2 + s], 0, 0, 0))
    return pl.pallas_call(
        functools.partial(attend_kernel, chunk, block_rows, devices),
        grid_spec=pltpu.PrefetchScalarGridSpec(
            num_scalar_prefetch=2,
            grid=(count,),
            in_specs=[
                rows,
                rows,
                kept,
                kept,
                pl.BlockSpec(
                    (fresh.shape[0], 2, 1, fresh.shape[3], HD), lambda s, m, n: (0, 0, s, 0, m[0])
                ),
            ],
            out_specs=pl.BlockSpec((1, blocks, part, width), lambda s, m, n: (s, 0, 0, 0)),
        ),
        out_shape=jax.ShapeDtypeStruct((count, blocks, part, width), bf16),
        compiler_params=pltpu.CompilerParams(vmem_limit_bytes=48 * 2**20),
        cost_estimate=pl.CostEstimate(flops=10**10, bytes_accessed=8 * 10**6, transcendentals=0),
        name="attend",
    )(scalars, lengths, q, gate, near, far, fresh)


def swap(x, devices, bit):
    return lax.ppermute(x, "head", [(h, h ^ bit) for h in range(devices)])


def halves(x, me, bit, lowest):
    split = x.reshape(x.shape[0] // (2 * lowest), 2, lowest, *x.shape[1:])
    mine = (me // bit) % 2

    def pick(which):
        got = lax.dynamic_index_in_dim(split, which, 1, keepdims=False)
        return got.reshape(x.shape[0] // 2, *x.shape[1:])

    return pick(mine), pick(1 - mine)


def add(a, b):
    return (a.astype(f32) + b.astype(f32)).astype(bf16)


def project(heads, weight, devices, me):
    bits = devices.bit_length() - 1
    kept, sent = halves(heads, me, 1, 1)

    def product(x):
        out = jnp.dot(x.reshape(-1, x.shape[2]), weight, preferred_element_type=f32)
        return out.astype(bf16).reshape(x.shape[0], x.shape[1], -1)

    arrived = swap(product(sent), devices, 1)
    total = add(product(kept), arrived)
    wide = total.shape[2] // 2
    done = []
    for side, order in enumerate((range(1, bits), range(bits - 1, 0, -1))):
        part = total[:, :, side * wide : (side + 1) * wide]
        left = list(range(1, bits))
        for bit in order:
            mine, other = halves(part, me, 1 << bit, 1 << left.index(bit))
            left.remove(bit)
            part = add(mine, swap(other, devices, 1 << bit))
        done.append(part[0])
    return jnp.concatenate(done, axis=1)


def on_device(
    delta_query,
    delta_key,
    delta_value,
    delta_gate,
    write_strength,
    decay_log,
    kept_state,
    kept_kv,
    fresh_kv,
    attn_query,
    attn_gate,
    cached_len,
    slot_of_session,
    delta_out_weight,
    attn_out_weight,
):
    count, fresh_len, query_cols = attn_query.shape
    owners = lax.axis_size("cache")
    devices = lax.axis_size("head")
    owner_id = lax.axis_index("cache")
    me = lax.axis_index("head")
    session_ids = jnp.arange(slot_of_session.shape[0], dtype=jnp.int32)
    on_mine = slot_of_session // count == owner_id
    owner_of = session_ids // count
    wanted = on_mine[None, :] & (owner_of[None, :] == jnp.arange(owners, dtype=jnp.int32)[:, None])
    picked_slot = jnp.sum(jnp.where(wanted, slot_of_session[None, :] - owner_id * count, 0), axis=1)
    my_slots = lax.dynamic_slice_in_dim(slot_of_session, owner_id * count, count)
    source = my_slots // count
    lengths = lax.dynamic_slice_in_dim(cached_len, owner_id * count, count)

    def exchange(x):
        return lax.all_to_all(x, "cache", split_axis=0, concat_axis=0, tiled=True)

    def pick(x):
        return jnp.concatenate([lax.dynamic_slice_in_dim(x, picked_slot[o], 1, 0) for o in range(owners)], axis=0)

    start = exchange(pick(kept_state).astype(bf16))
    landed = exchange(pick(kept_kv.transpose(0, 2, 1, 3)))

    heads_dev = query_cols // HD
    kv_head = me * heads_dev // (AH // KVH)
    fresh_all = lax.all_gather(fresh_kv.transpose(2, 0, 1, 3), "head", axis=0, tiled=False)

    own = lax.dynamic_slice_in_dim(landed, kv_head * HD, HD, 3)
    other = lax.dynamic_slice_in_dim(landed, (1 - kv_head) * HD, HD, 3)
    half = devices // 2
    near = jnp.stack([own, swap(other, devices, half)])
    bit = half // 2
    while bit > 1:
        near = jnp.concatenate([near, swap(near, devices, bit)], axis=0)
        bit //= 2
    far = swap(near, devices, 1)

    delta_heads, final_state = delta_layer(
        delta_query, delta_key, delta_value, delta_gate, write_strength, decay_log, start, source
    )
    block_rows = count * fresh_len // devices
    delta_mixed = project(delta_heads.reshape(devices, block_rows, -1), delta_out_weight, devices, me)

    scalars = jnp.stack([kv_head, me]).astype(jnp.int32)
    q4 = attn_query.reshape(count, fresh_len // block_rows, block_rows, query_cols)
    gate4 = attn_gate.reshape(q4.shape)
    done = []
    for chunk in range(CHUNKS):
        heads = attend(
            chunk, block_rows, devices, q4, gate4, near, far, fresh_all, scalars, lengths, source
        )
        heads = heads.reshape(devices, block_rows // CHUNKS, query_cols)
        done.append(project(heads, attn_out_weight, devices, me))
    return (delta_mixed, jnp.concatenate(done, axis=0), final_state)


def solution(mesh):
    in_specs = (
        P("cache", None, "head"),
        P("cache", None, "head"),
        P("cache", None, "head"),
        P("cache", None, "head"),
        P("cache", "head", None),
        P("cache", "head", None),
        P("cache", "head", None, None),
        P("cache", "head", None, None),
        P("cache", "head", None, None),
        P("cache", None, "head"),
        P("cache", None, "head"),
        P(),
        P(),
        P("head", None),
        P("head", None),
    )
    out_specs = (
        P(("cache", "head"), None),
        P(("cache", "head"), None),
        P("cache", "head", None, None),
    )
    return jax.shard_map(
        on_device, mesh=mesh, in_specs=in_specs, out_specs=out_specs, check_vma=False
    )
```

profile of v0, /device:TPU:0, one launch (start us, length us, event | category | flops | bytes accessed | tf_op | source)
XLA Modules:
  0.0 277.2 jit_solution(9708476051499770681)
XLA Ops:
  7.2 0.8 fusion.16
  8.0 0.7 and_select_fusion
  8.8 0.7 fusion.20
  17.2 1.3 dynamic-slice_convert_fusion.3
  18.5 0.9 pad_maximum_fusion.4
  19.3 6.3 %all-to-all-start = ((bf16[4,4,128,128]{3,2,1,0:T(8,128)(2,1)}), bf16[4,4,128,128]{3,2,1,0:T(8,128)(2,1)}, u32[]{:S(2)}, u32[]{:S(2)}) async-start(bf16[4,4,128,128]{3,2,1,0:T(8,128)(2,1)} %pad_maximum_fusion.4), calls=%async_computation | async-start | bytes 1048576 | tf_op jit(solution)/shard_map/all_to_all | solution.py:289
  25.7 4.8 %reduce_window_sum.11 = f32[4,4,4,128]{3,2,1,0:T(4,128)S(1)} reduce-window(f32[4,4,4,128]{3,2,1,0:T(4,128)S(1)} %reshape.198, f32[]{:T(128)} %constant.242.clone.1), window={size=1x1x1x128 pad=0_0x0_0x0_0x127_0}, to_apply=%region_0.1 | reduce-window | flops 1040384 | bytes 65540 | tf_op jit(solution)/shard_map/jit(cumsum)/reduce_window_sum | solution.py:97
  31.0 9.2 %all-to-all-done.start_ref = bf16[4,4,128,128]{3,2,1,0:T(8,128)(2,1)} async-done(((bf16[4,4,128,128]{3,2,1,0:T(8,128)(2,1)}), bf16[4,4,128,128]{3,2,1,0:T(8,128)(2,1)}, u32[]{:S(2)}, u32[]{:S(2)}) %all-to-all-start) | async-done | bytes 524320 | tf_op jit(solution)/shard_map/all_to_all | solution.py:289
  40.3 1.6 copy-done.2
  41.8 1.6 copy-done.3
  43.4 1.2 copy-done.6
  44.7 1.2 copy-done.7
  45.9 36.0 %delta_layer.1 = (bf16[4,512,512]{2,1,0:T(8,128)(2,1)S(1)}, f32[4,4,128,128]{3,2,1,0:T(8,128)}) custom-call(s32[4]{0:T(128)S(1)} %and_select_fusion.2.source, bf16[4,512,256]{2,1,0:T(8,128)(2,1)S(1)} %copy-done.6, bf16[4,512,256]{2,1,0:T(8,128)(2,1)S(1)} %copy-done.7, bf16[4,512,512]{2,1,0:T(8,128)(2,1)S(1)} %copy-done.2, ...), custom_call_target="tpu_custom_call" | custom-call | flops 40000000000 | bytes 12000000 | tf_op jit(solution)/shard_map/delta_layer/pallas_call | solution.py:104
  81.9 1.2 constant_dynamic-slice_fusion.15
  83.1 4.4 %convolution_convert_fusion = bf16[1024,2048]{1,0:T(8,128)(2,1)} fusion(bf16[1024,512]{1,0:T(8,128)(2,1)S(1)} %bitcast.131, bf16[512,2048]{1,0:T(8,128)(2,1)S(1)} %copy-done), kind=kOutput, calls=%fused_computation.6 | convolution fusion | flops 2149580800 | bytes 7340032 | tf_op jit(solution)/shard_map/dot_general | solution.py:239
  87.4 0.9 copy.59
  88.9 0.7 constant_dynamic-slice_fusion.12
  89.7 1.1 pad_maximum_fusion.2
  90.8 4.4 %all-to-all-start.1 = ((bf16[4,2,128,512]{3,2,1,0:T(8,128)(2,1)}), bf16[4,2,128,512]{3,2,1,0:T(8,128)(2,1)}, u32[]{:S(2)}, u32[]{:S(2)}) async-start(bf16[4,2,128,512]{3,2,1,0:T(8,128)(2,1)} %pad_maximum_fusion.2), calls=%async_computation.1 | async-start | bytes 2097152 | tf_op jit(solution)/shard_map/all_to_all | solution.py:289
  95.3 26.1 %all-to-all-done.1 = bf16[4,2,128,512]{3,2,1,0:T(8,128)(2,1)} async-done(((bf16[4,2,128,512]{3,2,1,0:T(8,128)(2,1)}), bf16[4,2,128,512]{3,2,1,0:T(8,128)(2,1)}, u32[]{:S(2)}, u32[]{:S(2)}) %all-to-all-start.1) | async-done | bytes 1048608 | tf_op jit(solution)/shard_map/all_to_all | solution.py:289
  121.4 2.1 dynamic-slice_bitcast_fusion.6
  123.4 1.5 collective-permute-start.5
  124.9 3.6 %convolution_convert_fusion.1 = bf16[1024,2048]{1,0:T(8,128)(2,1)S(1)} fusion(bf16[1024,512]{1,0:T(8,128)(2,1)} %bitcast.130, bf16[512,2048]{1,0:T(8,128)(2,1)S(1)} %copy-done), kind=kOutput, calls=%fused_computation.7 | convolution fusion | flops 2149580800 | bytes 7340032 | tf_op jit(solution)/shard_map/dot_general | solution.py:239
  128.5 8.2 %collective-permute-done.5 = bf16[4,2,128,256]{3,2,1,0:T(8,128)(2,1)S(1)} collective-permute-done((bf16[4,2,128,256]{3,2,1,0:T(8,128)(2,1)}, bf16[4,2,128,256]{3,2,1,0:T(8,128)(2,1)S(1)}, u32[]{:S(2)}, u32[]{:S(2)}) %collective-permute-start.5) | collective-permute-done | bytes 524320 | tf_op jit(solution)/shard_map/ppermute | solution.py:216
  136.7 1.1 pad_maximum_fusion.3
  137.7 1.5 collective-permute-start.6
  139.2 4.1 %fusion = bf16[4,256,2048]{2,1,0:T(8,128)(2,1)S(1)} fusion(bf16[4,256,2048]{2,1,0:T(8,128)(2,1)S(1)} %bitcast.116, bf16[4,256,2048]{2,1,0:T(8,128)(2,1)} %collective-permute-done), kind=kLoop, calls=%fused_computation.1 | loop fusion | flops 8388608 | bytes 12582912 | tf_op jit(solution)/shard_map/convert_element_type | solution.py:231
  143.8 1.3 copy-done.8
  145.1 1.0 dynamic-slice_bitcast_fusion.1
  146.7 1.0 dynamic-slice_bitcast_fusion
  147.7 1.5 collective-permute-start.3
  149.3 14.9 %collective-permute-done.6 = bf16[2,4,2,128,256]{4,3,2,1,0:T(8,128)(2,1)} collective-permute-done((bf16[2,4,2,128,256]{4,3,2,1,0:T(8,128)(2,1)}, bf16[2,4,2,128,256]{4,3,2,1,0:T(8,128)(2,1)}, u32[]{:S(2)}, u32[]{:S(2)}) %collective-permute-start.6) | collective-permute-done | bytes 1048608 | tf_op jit(solution)/shard_map/ppermute | solution.py:216
  164.1 2.8 %pad_maximum_fusion.near_ref = bf16[4,4,2,128,256]{4,3,2,1,0:T(8,128)(2,1)} fusion(bf16[2,4,2,128,256]{4,3,2,1,0:T(8,128)(2,1)} %collective-permute-done.6, bf16[1,4,2,128,256]{4,3,2,1,0:T(8,128)(2,1)S(1)} %bitcast.129, bf16[1,4,2,128,256]{4,3,2,1,0:T(8,128)(2,1)S(1)} %get-tuple-element.19), kind=kLoop, calls=%fused_computation.12 | loop fusion | flops 2097152 | bytes 4194304 | tf_op jit(solution)/shard_map/concatenate | solution.py:307
  166.9 16.9 %collective-permute-done.1 = bf16[2,256,1024]{2,1,0:T(8,128)(2,1)} collective-permute-done((bf16[2,256,1024]{2,1,0:T(8,128)(2,1)}, bf16[2,256,1024]{2,1,0:T(8,128)(2,1)}, u32[]{:S(2)}, u32[]{:S(2)}) %collective-permute-start.1) | collective-permute-done | bytes 1048608 | tf_op jit(solution)/shard_map/ppermute | solution.py:216
  183.9 1.9 fusion.4
  185.9 1.6 collective-permute-start.2
  187.5 1.6 fusion.3
  189.2 1.6 collective-permute-start.4
  190.9 6.2 %collective-permute-done.2 = bf16[1,256,1024]{2,1,0:T(8,128)(2,1)S(1)} collective-permute-done((bf16[1,256,1024]{2,1,0:T(8,128)(2,1)S(1)}, bf16[1,256,1024]{2,1,0:T(8,128)(2,1)S(1)}, u32[]{:S(2)}, u32[]{:S(2)}) %collective-permute-start.2) | collective-permute-done | bytes 524320 | tf_op jit(solution)/shard_map/ppermute | solution.py:216
  197.3 2.8 %collective-permute-done.4 = bf16[1,256,1024]{2,1,0:T(8,128)(2,1)S(1)} collective-permute-done((bf16[1,256,1024]{2,1,0:T(8,128)(2,1)S(1)}, bf16[1,256,1024]{2,1,0:T(8,128)(2,1)S(1)}, u32[]{:S(2)}, u32[]{:S(2)}) %collective-permute-start.4) | collective-permute-done | bytes 524320 | tf_op jit(solution)/shard_map/ppermute | solution.py:216
  200.4 1.6 copy-done.5
  202.0 9.8 %attend.2 = bf16[4,2,128,512]{3,2,1,0:T(8,128)(2,1)S(1)} custom-call(s32[6]{0:T(128)S(1)} %pad_add_fusion.scalars, s32[4]{0:T(128)S(1)} %dynamic_slice.141.lengths, bf16[4,2,256,512]{3,2,1,0:T(8,128)(2,1)S(1)} %bitcast.108, bf16[4,2,256,512]{3,2,1,0:T(8,128)(2,1)S(1)} %bitcast.110, bf16[4,4,2,128,256]{4,3,2,1,0:T(8,128)(2,1)} %pad_maximum_fusion.near_ref, ...), custom_call_target="tpu_custom_call" | custom-call | flops 10000000000 | bytes 8000000 | tf_op jit(solution)/shard_map/attend/pallas_call | solution.py:192
  211.9 1.5 copy-done.14
  213.4 1.3 convolution_convert_fusion.4
  214.8 10.1 %attend.3 = bf16[4,2,128,512]{3,2,1,0:T(8,128)(2,1)S(1)} custom-call(s32[6]{0:T(128)S(1)} %pad_add_fusion.scalars, s32[4]{0:T(128)S(1)} %dynamic_slice.141.lengths, bf16[4,2,256,512]{3,2,1,0:T(8,128)(2,1)S(1)} %bitcast.109, bf16[4,2,256,512]{3,2,1,0:T(8,128)(2,1)S(1)} %bitcast.111, bf16[4,4,2,128,256]{4,3,2,1,0:T(8,128)(2,1)} %pad_maximum_fusion.near_ref, ...), custom_call_target="tpu_custom_call" | custom-call | flops 10000000000 | bytes 8000000 | tf_op jit(solution)/shard_map/attend/pallas_call | solution.py:192
  224.9 1.3 convolution_convert_fusion.2
  226.2 0.6 collective-permute-start.13
  226.8 1.1 pad_maximum_fusion.1
  227.8 1.3 convolution_convert_fusion.5
  229.1 1.3 convolution_convert_fusion.3
  230.4 0.8 fusion.2
  231.4 1.6 collective-permute-start.9
  233.5 0.9 fusion.1
  234.7 0.6 collective-permute-start.14
  235.3 1.6 collective-permute-start.16
  236.9 9.3 %collective-permute-done.9 = bf16[2,128,1024]{2,1,0:T(8,128)(2,1)S(1)} collective-permute-done((bf16[2,128,1024]{2,1,0:T(8,128)(2,1)S(1)}, bf16[2,128,1024]{2,1,0:T(8,128)(2,1)S(1)}, u32[]{:S(2)}, u32[]{:S(2)}) %collective-permute-start.9) | collective-permute-done | bytes 524320 | tf_op jit(solution)/shard_map/ppermute | solution.py:216
  247.0 0.9 collective-permute-done.11
  248.2 0.7 collective-permute-start.12
  248.8 8.7 %collective-permute-done.14 = bf16[2,128,1024]{2,1,0:T(8,128)(2,1)S(1)} collective-permute-done((bf16[2,128,1024]{2,1,0:T(8,128)(2,1)S(1)}, bf16[2,128,1024]{2,1,0:T(8,128)(2,1)S(1)}, u32[]{:S(2)}, u32[]{:S(2)}) %collective-permute-start.14) | collective-permute-done | bytes 524320 | tf_op jit(solution)/shard_map/ppermute | solution.py:216
  258.3 0.9 collective-permute-done.16
  259.4 0.7 collective-permute-start.17
  260.1 4.7 %collective-permute-done.10 = bf16[1,128,1024]{2,1,0:T(8,128)(2,1)S(1)} collective-permute-done((bf16[1,128,1024]{2,1,0:T(8,128)(2,1)S(1)}, bf16[1,128,1024]{2,1,0:T(8,128)(2,1)S(1)}, u32[]{:S(2)}, u32[]{:S(2)}) %collective-permute-start.10) | collective-permute-done | bytes 262176 | tf_op jit(solution)/shard_map/ppermute | solution.py:216
  264.9 4.2 %collective-permute-done.15 = bf16[1,128,1024]{2,1,0:T(8,128)(2,1)S(1)} collective-permute-done((bf16[1,128,1024]{2,1,0:T(8,128)(2,1)S(1)}, bf16[1,128,1024]{2,1,0:T(8,128)(2,1)S(1)}, u32[]{:S(2)}, u32[]{:S(2)}) %collective-permute-start.15) | collective-permute-done | bytes 262176 | tf_op jit(solution)/shard_map/ppermute | solution.py:216
  269.3 1.1 maximum_maximum_fusion
  (79 shorter events, 6.5 us)
Async XLA Ops:
  7.2 75.9 %copy-start = (bf16[512,2048]{1,0:T(8,128)(2,1)S(1)}, bf16[512,2048]{1,0:T(8,128)(2,1)}, u32[]{:S(2)}) copy-start(bf16[512,2048]{1,0:T(8,128)(2,1)} %param.28) | copy-start | bytes 6291460
  7.2 18.5 %copy-start.11 = (f32[4,4,512]{2,1,0:T(4,128)S(1)}, f32[4,4,512]{2,1,0:T(4,128)}, u32[]{:S(2)}) copy-start(f32[4,4,512]{2,1,0:T(4,128)} %param.20) | copy-start | bytes 98308
  7.2 23.4 %copy-start.12 = (f32[4,4,512]{2,1,0:T(4,128)S(1)}, f32[4,4,512]{2,1,0:T(4,128)}, u32[]{:S(2)}) copy-start(f32[4,4,512]{2,1,0:T(4,128)} %param.19) | copy-start | bytes 98308
  17.2 13.8 %copy-start.13 = (s32[16]{0:T(128)S(1)}, s32[16]{0:T(128)}, u32[]{:S(2)}) copy-start(s32[16]{0:T(128)} %param.27) | copy-start | bytes 196
  19.3 20.9 %all-to-all-start = ((bf16[4,4,128,128]{3,2,1,0:T(8,128)(2,1)}), bf16[4,4,128,128]{3,2,1,0:T(8,128)(2,1)}, u32[]{:S(2)}, u32[]{:S(2)}) async-start(bf16[4,4,128,128]{3,2,1,0:T(8,128)(2,1)} %pad_maximum_fusion.4), calls=%async_computation | async-start | bytes 1048576 | tf_op jit(solution)/shard_map/all_to_all | solution.py:289
  25.7 174.7 %all-gather.3.cloned.1.call-start = ((), (), s32[]{:S(2)}) async-start(), calls=%async_computation.2 | async-start | bytes 4718592 | tf_op jit(solution)/shard_map/all_gather | solution.py:299
  40.3 1.6 copy-start.2
  41.8 1.6 copy-start.3
  43.4 1.2 copy-start.6
  44.7 1.2 copy-start.7
  83.1 4.4 %copy-start.10 = (bf16[4,64,2,512]{3,2,1,0:T(2,128)(2,1)S(1)}, bf16[4,64,2,512]{3,2,1,0:T(2,128)(2,1)}, u32[]{:S(2)}) copy-start(bf16[4,64,2,512]{3,2,1,0:T(2,128)(2,1)} %param.23) | copy-start | bytes 1572868
  87.4 1.4 copy-start.9
  87.4 51.8 %collective-permute-start = (bf16[4,256,2048]{2,1,0:T(8,128)(2,1)}, bf16[4,256,2048]{2,1,0:T(8,128)(2,1)}, u32[]{:S(2)}, u32[]{:S(2)}) collective-permute-start(bf16[4,256,2048]{2,1,0:T(8,128)(2,1)} %bitcast.9), channel_id=1, source_target_pairs={{0,1},{1,0},{2,3},{3,2},{4,5},{5,4},{6,7},{7,6},{8,9},{9,8},{10,11... | collective-permute-start | bytes 12582920 | tf_op jit(solution)/shard_map/ppermute | solution.py:216
  90.8 30.5 %all-to-all-start.1 = ((bf16[4,2,128,512]{3,2,1,0:T(8,128)(2,1)}), bf16[4,2,128,512]{3,2,1,0:T(8,128)(2,1)}, u32[]{:S(2)}, u32[]{:S(2)}) async-start(bf16[4,2,128,512]{3,2,1,0:T(8,128)(2,1)} %pad_maximum_fusion.2), calls=%async_computation.1 | async-start | bytes 2097152 | tf_op jit(solution)/shard_map/all_to_all | solution.py:289
  123.4 13.2 %collective-permute-start.5 = (bf16[4,2,128,256]{3,2,1,0:T(8,128)(2,1)}, bf16[4,2,128,256]{3,2,1,0:T(8,128)(2,1)S(1)}, u32[]{:S(2)}, u32[]{:S(2)}) collective-permute-start(bf16[4,2,128,256]{3,2,1,0:T(8,128)(2,1)} %get-tuple-element.20), channel_id=1, source_target_pairs={{0,4},{1,5},{2,6},{3,7},{4,0},{5,1},{6,2},{7,3},{8,12},{9,13},{10,... | collective-permute-start | bytes 1572872 | tf_op jit(solution)/shard_map/ppermute | solution.py:216
  137.7 26.4 %collective-permute-start.6 = (bf16[2,4,2,128,256]{4,3,2,1,0:T(8,128)(2,1)}, bf16[2,4,2,128,256]{4,3,2,1,0:T(8,128)(2,1)}, u32[]{:S(2)}, u32[]{:S(2)}) collective-permute-start(bf16[2,4,2,128,256]{4,3,2,1,0:T(8,128)(2,1)} %pad_maximum_fusion.3), channel_id=1, source_target_pairs={{0,2},{1,3},{2,0},{3,1},{4,6},{5,7},{6,4},{7,5},{8,10},{9,11},{10,... | collective-permute-start | bytes 3145736 | tf_op jit(solution)/shard_map/ppermute | solution.py:216
  143.8 1.3 copy-start.8
  146.1 37.7 %collective-permute-start.1 = (bf16[2,256,1024]{2,1,0:T(8,128)(2,1)}, bf16[2,256,1024]{2,1,0:T(8,128)(2,1)}, u32[]{:S(2)}, u32[]{:S(2)}) collective-permute-start(bf16[2,256,1024]{2,1,0:T(8,128)(2,1)} %dynamic-slice_bitcast_fusion.1), channel_id=1, source_target_pairs={{0,2},{1,3},{2,0},{3,1},{4,6},{5,7},{6,4},{7,5},{8,10},{9,11},{10,... | collective-permute-start | bytes 3145736 | tf_op jit(solution)/shard_map/ppermute | solution.py:216
  147.7 39.7 %collective-permute-start.3 = (bf16[2,256,1024]{2,1,0:T(8,128)(2,1)}, bf16[2,256,1024]{2,1,0:T(8,128)(2,1)}, u32[]{:S(2)}, u32[]{:S(2)}) collective-permute-start(bf16[2,256,1024]{2,1,0:T(8,128)(2,1)} %dynamic-slice_bitcast_fusion), channel_id=1, source_target_pairs={{0,4},{1,5},{2,6},{3,7},{4,0},{5,1},{6,2},{7,3},{8,12},{9,13},{10,... | collective-permute-start | bytes 3145736 | tf_op jit(solution)/shard_map/ppermute | solution.py:216
  166.9 33.4 %collective-permute-start.7 = (bf16[4,4,2,128,256]{4,3,2,1,0:T(8,128)(2,1)}, bf16[4,4,2,128,256]{4,3,2,1,0:T(8,128)(2,1)}, u32[]{:S(2)}, u32[]{:S(2)}) collective-permute-start(bf16[4,4,2,128,256]{4,3,2,1,0:T(8,128)(2,1)} %pad_maximum_fusion.near_ref), channel_id=1, source_target_pairs={{0,1},{1,0},{2,3},{3,2},{4,5},{5,4},{6,7},{7,6},{8,9},{9,8},{10,11... | collective-permute-start | bytes 6291464 | tf_op jit(solution)/shard_map/ppermute | solution.py:216
  185.8 4.9 %copy-start.15 = (s32[16]{0:T(128)S(1)}, s32[16]{0:T(128)}, u32[]{:S(2)}) copy-start(s32[16]{0:T(128)} %param.26) | copy-start | bytes 196
  185.9 11.2 %collective-permute-start.2 = (bf16[1,256,1024]{2,1,0:T(8,128)(2,1)S(1)}, bf16[1,256,1024]{2,1,0:T(8,128)(2,1)S(1)}, u32[]{:S(2)}, u32[]{:S(2)}) collective-permute-start(bf16[1,256,1024]{2,1,0:T(8,128)(2,1)S(1)} %constant_dynamic-slice_fusion.14), channel_id=1, source_target_pairs={{0,4},{1,5},{2,6},{3,7},{4,0},{5,1},{6,2},{7,3},{8,12},{9,13},{10,... | collective-permute-start | bytes 1572872 | tf_op jit(solution)/shard_map/ppermute | solution.py:216
  189.1 11.3 %copy-start.4 = (bf16[4,512,512]{2,1,0:T(8,128)(2,1)S(1)}, bf16[4,512,512]{2,1,0:T(8,128)(2,1)}, u32[]{:S(2)}) copy-start(bf16[4,512,512]{2,1,0:T(8,128)(2,1)} %param.24) | copy-start | bytes 6291460
  189.2 11.0 %collective-permute-start.4 = (bf16[1,256,1024]{2,1,0:T(8,128)(2,1)S(1)}, bf16[1,256,1024]{2,1,0:T(8,128)(2,1)S(1)}, u32[]{:S(2)}, u32[]{:S(2)}) collective-permute-start(bf16[1,256,1024]{2,1,0:T(8,128)(2,1)S(1)} %constant_dynamic-slice_fusion.13), channel_id=1, source_target_pairs={{0,2},{1,3},{2,0},{3,1},{4,6},{5,7},{6,4},{7,5},{8,10},{9,11},{10,... | collective-permute-start | bytes 1572872 | tf_op jit(solution)/shard_map/ppermute | solution.py:216
  200.4 1.6 copy-start.5
  211.8 1.6 copy-start.14
  214.7 15.7 %collective-permute-start.8 = (bf16[4,128,2048]{2,1,0:T(8,128)(2,1)S(1)}, bf16[4,128,2048]{2,1,0:T(8,128)(2,1)S(1)}, u32[]{:S(2)}, u32[]{:S(2)}) collective-permute-start(bf16[4,128,2048]{2,1,0:T(8,128)(2,1)S(1)} %bitcast.143), channel_id=1, source_target_pairs={{0,1},{1,0},{2,3},{3,2},{4,5},{5,4},{6,7},{7,6},{8,9},{9,8},{10,11... | collective-permute-start | bytes 6291464 | tf_op jit(solution)/shard_map/ppermute | solution.py:216
  226.2 7.3 %collective-permute-start.13 = (bf16[4,128,2048]{2,1,0:T(8,128)(2,1)S(1)}, bf16[4,128,2048]{2,1,0:T(8,128)(2,1)S(1)}, u32[]{:S(2)}, u32[]{:S(2)}) collective-permute-start(bf16[4,128,2048]{2,1,0:T(8,128)(2,1)S(1)} %bitcast.142), channel_id=1, source_target_pairs={{0,1},{1,0},{2,3},{3,2},{4,5},{5,4},{6,7},{7,6},{8,9},{9,8},{10,11... | collective-permute-start | bytes 6291464 | tf_op jit(solution)/shard_map/ppermute | solution.py:216
  231.4 14.8 %collective-permute-start.9 = (bf16[2,128,1024]{2,1,0:T(8,128)(2,1)S(1)}, bf16[2,128,1024]{2,1,0:T(8,128)(2,1)S(1)}, u32[]{:S(2)}, u32[]{:S(2)}) collective-permute-start(bf16[2,128,1024]{2,1,0:T(8,128)(2,1)S(1)} %dynamic-slice_bitcast_fusion.5), channel_id=1, source_target_pairs={{0,2},{1,3},{2,0},{3,1},{4,6},{5,7},{6,4},{7,5},{8,10},{9,11},{10,... | collective-permute-start | bytes 1572872 | tf_op jit(solution)/shard_map/ppermute | solution.py:216
  233.0 14.9 %collective-permute-start.11 = (bf16[2,128,1024]{2,1,0:T(8,128)(2,1)S(1)}, bf16[2,128,1024]{2,1,0:T(8,128)(2,1)S(1)}, u32[]{:S(2)}, u32[]{:S(2)}) collective-permute-start(bf16[2,128,1024]{2,1,0:T(8,128)(2,1)S(1)} %dynamic-slice_bitcast_fusion.4), channel_id=1, source_target_pairs={{0,4},{1,5},{2,6},{3,7},{4,0},{5,1},{6,2},{7,3},{8,12},{9,13},{10,... | collective-permute-start | bytes 1572872 | tf_op jit(solution)/shard_map/ppermute | solution.py:216
  234.7 22.8 %collective-permute-start.14 = (bf16[2,128,1024]{2,1,0:T(8,128)(2,1)S(1)}, bf16[2,128,1024]{2,1,0:T(8,128)(2,1)S(1)}, u32[]{:S(2)}, u32[]{:S(2)}) collective-permute-start(bf16[2,128,1024]{2,1,0:T(8,128)(2,1)S(1)} %dynamic-slice_bitcast_fusion.3), channel_id=1, source_target_pairs={{0,2},{1,3},{2,0},{3,1},{4,6},{5,7},{6,4},{7,5},{8,10},{9,11},{10,... | collective-permute-start | bytes 1572872 | tf_op jit(solution)/shard_map/ppermute | solution.py:216
  235.3 23.8 %collective-permute-start.16 = (bf16[2,128,1024]{2,1,0:T(8,128)(2,1)S(1)}, bf16[2,128,1024]{2,1,0:T(8,128)(2,1)S(1)}, u32[]{:S(2)}, u32[]{:S(2)}) collective-permute-start(bf16[2,128,1024]{2,1,0:T(8,128)(2,1)S(1)} %dynamic-slice_bitcast_fusion.2), channel_id=1, source_target_pairs={{0,4},{1,5},{2,6},{3,7},{4,0},{5,1},{6,2},{7,3},{8,12},{9,13},{10,... | collective-permute-start | bytes 1572872 | tf_op jit(solution)/shard_map/ppermute | solution.py:216
  246.5 18.3 %collective-permute-start.10 = (bf16[1,128,1024]{2,1,0:T(8,128)(2,1)S(1)}, bf16[1,128,1024]{2,1,0:T(8,128)(2,1)S(1)}, u32[]{:S(2)}, u32[]{:S(2)}) collective-permute-start(bf16[1,128,1024]{2,1,0:T(8,128)(2,1)S(1)} %constant_dynamic-slice_fusion.5), channel_id=1, source_target_pairs={{0,4},{1,5},{2,6},{3,7},{4,0},{5,1},{6,2},{7,3},{8,12},{9,13},{10,... | collective-permute-start | bytes 786440 | tf_op jit(solution)/shard_map/ppermute | solution.py:216
  248.2 16.7 %collective-permute-start.12 = (bf16[1,128,1024]{2,1,0:T(8,128)(2,1)S(1)}, bf16[1,128,1024]{2,1,0:T(8,128)(2,1)S(1)}, u32[]{:S(2)}, u32[]{:S(2)}) collective-permute-start(bf16[1,128,1024]{2,1,0:T(8,128)(2,1)S(1)} %constant_dynamic-slice_fusion.4), channel_id=1, source_target_pairs={{0,2},{1,3},{2,0},{3,1},{4,6},{5,7},{6,4},{7,5},{8,10},{9,11},{10,... | collective-permute-start | bytes 786440 | tf_op jit(solution)/shard_map/ppermute | solution.py:216
  257.7 11.4 %collective-permute-start.15 = (bf16[1,128,1024]{2,1,0:T(8,128)(2,1)S(1)}, bf16[1,128,1024]{2,1,0:T(8,128)(2,1)S(1)}, u32[]{:S(2)}, u32[]{:S(2)}) collective-permute-start(bf16[1,128,1024]{2,1,0:T(8,128)(2,1)S(1)} %constant_dynamic-slice_fusion.1), channel_id=1, source_target_pairs={{0,4},{1,5},{2,6},{3,7},{4,0},{5,1},{6,2},{7,3},{8,12},{9,13},{10,... | collective-permute-start | bytes 786440 | tf_op jit(solution)/shard_map/ppermute | solution.py:216
  259.4 9.8 %collective-permute-start.17 = (bf16[1,128,1024]{2,1,0:T(8,128)(2,1)S(1)}, bf16[1,128,1024]{2,1,0:T(8,128)(2,1)S(1)}, u32[]{:S(2)}, u32[]{:S(2)}) collective-permute-start(bf16[1,128,1024]{2,1,0:T(8,128)(2,1)S(1)} %constant_dynamic-slice_fusion), channel_id=1, source_target_pairs={{0,2},{1,3},{2,0},{3,1},{4,6},{5,7},{6,4},{7,5},{8,10},{9,11},{10,... | collective-permute-start | bytes 786440 | tf_op jit(solution)/shard_map/ppermute | solution.py:216
  264.8 5.6 %copy-start.1 = (bf16[512,2048]{1,0:T(8,128)(2,1)S(1)}, bf16[512,2048]{1,0:T(8,128)(2,1)}, u32[]{:S(2)}) copy-start(bf16[512,2048]{1,0:T(8,128)(2,1)} %param.28) | copy-start | bytes 6291460
Sparse Core Ops, SparseCore 0:
  88.5 35.9 all-gather.2
where the time goes:
time: 278 us; the launch traced here: 277 us
  waiting for transfers between devices  113 us (41%)
  Pallas kernels  55.9 us (20%)
  starting transfers between devices  26.3 us (9%)
  other arithmetic  25.4 us (9%)
  between operations  22.3 us (8%)
  local copies, waits for them, and re-layouts  21.4 us (8%)
  matrix products  13 us (5%)
    ppermute x18, waiting for transfers between devices, swap(): return lax.ppermute(x, 'head', [(h, h ^ bit) for h in range(devices)])  77.7 us
    pallas_call x1, Pallas kernels, delta_layer(): pl.pallas_call(delta_kernel, grid_spec=pltpu.PrefetchScalarGridSpec(num_s...  36 us
    all_to_all x2, waiting for transfers between devices, exchange(): return lax.all_to_all(x, 'cache', split_axis=0, concat_axis=0, tiled=True)  35.3 us
    pallas_call x2, Pallas kernels, attend(): pl.pallas_call(functools.partial(attend_kernel, chunk, block_rows, device...  19.9 us
    ppermute x18, starting transfers between devices, swap(): return lax.ppermute(x, 'head', [(h, h ^ bit) for h in range(devices)])  15.6 us
    dot_general x6, matrix products, product(): out = jnp.dot(x.reshape(-1, x.shape[2]), weight, preferred_element_type=f32)  13 us
    unnamed x37, local copies, waits for them, and re-layouts  11.6 us
    all_to_all x2, starting transfers between devices, exchange(): return lax.all_to_all(x, 'cache', split_axis=0, concat_axis=0, tiled=True)  10.7 us
  transfers between devices with their start and end apart: 21, of which 13 were waited for; matrix products, arithmetic and copies ran while one was open for 13% of the time, Pallas kernels for 4%

commit v1 on v0

--- a/solution.py
+++ b/solution.py
@@ -15,6 +15,7 @@
 HD = 256
 BLOCK = 128
 PAIR = 2
+PARTS = 2
 CHUNKS = 2
 
 big_negative = -1e30
@@ -26,17 +27,17 @@
     return lax.dot_general(a, b, (dims, ((), ())), preferred_element_type=f32)
 
 
-def delta_kernel(source, q_ref, k_ref, v_ref, gate_ref, row_ref, col_ref, start_ref, heads_ref, state_ref):
-    pair = pl.program_id(0)
+def delta_kernel(deps, source, q_ref, k_ref, v_ref, gate_ref, row_ref, col_ref, start_ref, *refs):
+    heads_ref, state_ref = refs[deps:]
     sessions, _, q_cols = q_ref.shape
     key_heads = q_cols // LK
     value_heads = v_ref.shape[2] // LV
     ratio = value_heads // key_heads
 
-    @pl.when(pl.program_id(1) == 0)
+    @pl.when(pl.program_id(0) == 0)
     def _():
         for s in range(sessions):
-            state_ref[s] = start_ref[source[pair * sessions + s]].astype(f32)
+            state_ref[s] = start_ref[source[s]].astype(f32)
 
     rows = lax.broadcasted_iota(jnp.int32, (BLOCK, BLOCK), 0)
     cols = lax.broadcasted_iota(jnp.int32, (BLOCK, BLOCK), 1)
@@ -91,46 +92,56 @@
         heads_ref[s, :, j * LV : (j + 1) * LV] = (emitted * scale * (gate / (1.0 + jnp.exp(-gate)))).astype(bf16)
 
 
-def delta_layer(q, k, v, gate, strength, decay, start, source):
+def block_rates(strength, decay):
+    count, value_heads, fresh_len = decay.shape
+    upto = jnp.triu(jnp.ones((BLOCK, BLOCK), f32))
+    running = jnp.matmul(decay.reshape(-1, BLOCK), upto, precision=lax.Precision.HIGHEST)
+    running = running.reshape(count, value_heads, fresh_len)
+    return running, jnp.concatenate([running, strength], axis=1).transpose(0, 2, 1)
+
+
+def delta_part(q, k, v, gate, running, columns, start, places, heads, pair, part, deps):
     count, fresh_len, value_cols = v.shape
     value_heads = value_cols // LV
-    running = jnp.cumsum(decay.reshape(count, value_heads, fresh_len // BLOCK, BLOCK), axis=-1)
-    running = running.reshape(count, value_heads, fresh_len)
-    columns = jnp.concatenate([running, strength], axis=1).transpose(0, 2, 1)
+    steps = fresh_len // BLOCK // PARTS
+    unread = ([] if heads is None else [heads]) + list(deps)
 
     def rows(width):
-        return pl.BlockSpec((PAIR, BLOCK, width), lambda s, c, _: (s, c, 0))
+        return pl.BlockSpec((PAIR, BLOCK, width), lambda c, _: (pair, part * steps + c, 0))
 
     return pl.pallas_call(
-        delta_kernel,
+        functools.partial(delta_kernel, len(unread)),
         grid_spec=pltpu.PrefetchScalarGridSpec(
             num_scalar_prefetch=1,
-            grid=(count // PAIR, fresh_len // BLOCK),
+            grid=(steps,),
             in_specs=[
                 rows(q.shape[2]),
                 rows(k.shape[2]),
                 rows(value_cols),
                 rows(value_cols),
-                pl.BlockSpec((PAIR, value_heads, BLOCK), lambda s, c, _: (s, 0, c)),
+                pl.BlockSpec((PAIR, value_heads, BLOCK), lambda c, _: (pair, 0, part * steps + c)),
                 rows(2 * value_heads),
-                pl.BlockSpec(start.shape, lambda s, c, _: (0, 0, 0, 0)),
-            ],
+                pl.BlockSpec(start.shape, lambda c, _: (0, 0, 0, 0)),
+            ]
+            + [pl.BlockSpec(memory_space=pl.ANY)] * len(unread),
             out_specs=[
                 rows(value_cols),
-                pl.BlockSpec((PAIR, value_heads, LK, LV), lambda s, c, _: (s, 0, 0, 0)),
+                pl.BlockSpec((PAIR, value_heads, LK, LV), lambda c, _: (0, 0, 0, 0)),
             ],
         ),
         out_shape=[
             jax.ShapeDtypeStruct((count, fresh_len, value_cols), bf16),
-            jax.ShapeDtypeStruct((count, value_heads, LK, LV), f32),
+            jax.ShapeDtypeStruct((PAIR, value_heads, LK, LV), f32),
         ],
-        compiler_params=pltpu.CompilerParams(vmem_limit_bytes=40 * 2**20),
-        cost_estimate=pl.CostEstimate(flops=4 * 10**10, bytes_accessed=12 * 10**6, transcendentals=0),
-        name="delta_layer",
-    )(source, q, k, v, gate, running, columns, start)
-
-
-def attend_kernel(chunk, block_rows, devices, scalars, lengths, q_ref, gate_ref, near_ref, far_ref, fresh_ref, out_ref):
+        input_output_aliases={} if heads is None else {8: 0},
+        compiler_params=pltpu.CompilerParams(vmem_limit_bytes=32 * 2**20),
+        cost_estimate=pl.CostEstimate(flops=10**10, bytes_accessed=3 * 10**6, transcendentals=0),
+        name="delta_part",
+    )(places, q, k, v, gate, running, columns, start, *unread)
+
+
+def attend_kernel(chunk, block_rows, devices, scalars, lengths, q_ref, gate_ref, near_ref, far_ref, fresh_ref, *refs):
+    out_ref = refs[-1]
     s = pl.program_id(0)
     me = scalars[1]
     length = lengths[s]
@@ -182,10 +193,10 @@
         out_ref[0, :, :, h * HD : (h + 1) * HD] = gated.astype(bf16).reshape(blocks, part, HD)
 
 
-def attend(chunk, block_rows, devices, q, gate, near, far, fresh, scalars, lengths, source):
+def attend(chunk, block_rows, devices, q, gate, near, far, fresh, scalars, lengths, places, deps):
     count, blocks, _, width = q.shape
     part = block_rows // CHUNKS
-    scalars = jnp.concatenate([scalars, source])
+    scalars = jnp.concatenate([scalars, places])
     slots, _, _, kept_rows, _ = near.shape
     rows = pl.BlockSpec((1, blocks, part, width), lambda s, m, n: (s, 0, chunk, 0))
     kept = pl.BlockSpec((slots, 1, 2, kept_rows, HD), lambda s, m, n: (0, m[2 + s], 0, 0, 0))
@@ -202,18 +213,19 @@
                 pl.BlockSpec(
                     (fresh.shape[0], 2, 1, fresh.shape[3], HD), lambda s, m, n: (0, 0, s, 0, m[0])
                 ),
-            ],
+            ]
+            + [pl.BlockSpec(memory_space=pl.ANY)] * len(deps),
             out_specs=pl.BlockSpec((1, blocks, part, width), lambda s, m, n: (s, 0, 0, 0)),
         ),
         out_shape=jax.ShapeDtypeStruct((count, blocks, part, width), bf16),
         compiler_params=pltpu.CompilerParams(vmem_limit_bytes=48 * 2**20),
         cost_estimate=pl.CostEstimate(flops=10**10, bytes_accessed=8 * 10**6, transcendentals=0),
         name="attend",
-    )(scalars, lengths, q, gate, near, far, fresh)
-
-
-def swap(x, devices, bit):
-    return lax.ppermute(x, "head", [(h, h ^ bit) for h in range(devices)])
+    )(scalars, lengths, q, gate, near, far, fresh, *deps)
+
+
+def swap(x, devices, bit, axis="head"):
+    return lax.ppermute(x, axis, [(h, h ^ bit) for h in range(devices)])
 
 
 def halves(x, me, bit, lowest):
@@ -231,27 +243,38 @@
     return (a.astype(f32) + b.astype(f32)).astype(bf16)
 
 
-def project(heads, weight, devices, me):
+def product(x, weight):
+    out = jnp.dot(x.reshape(-1, x.shape[2]), weight, preferred_element_type=f32)
+    return out.astype(bf16).reshape(x.shape[0], x.shape[1], -1)
+
+
+def project_first(heads, weight, devices, me):
+    kept, sent = halves(heads, me, 1, 1)
+    return add(product(kept, weight), swap(product(sent, weight), devices, 1))
+
+
+def project_next(parts, devices, me):
     bits = devices.bit_length() - 1
-    kept, sent = halves(heads, me, 1, 1)
-
-    def product(x):
-        out = jnp.dot(x.reshape(-1, x.shape[2]), weight, preferred_element_type=f32)
-        return out.astype(bf16).reshape(x.shape[0], x.shape[1], -1)
-
-    arrived = swap(product(sent), devices, 1)
-    total = add(product(kept), arrived)
+    orders = (list(range(1, bits)), list(range(bits - 1, 0, -1)))
+    done = []
+    for part, order in zip(parts, orders):
+        left = part.shape[0].bit_length() - 1
+        bit = order[bits - 1 - left]
+        below = sum(1 for b in order[bits - 1 - left :] if b < bit)
+        mine, other = halves(part, me, 1 << bit, 1 << below)
+        done.append(add(mine, swap(other, devices, 1 << bit)))
+    return done
+
+
+def column_halves(total):
     wide = total.shape[2] // 2
-    done = []
-    for side, order in enumerate((range(1, bits), range(bits - 1, 0, -1))):
-        part = total[:, :, side * wide : (side + 1) * wide]
-        left = list(range(1, bits))
-        for bit in order:
-            mine, other = halves(part, me, 1 << bit, 1 << left.index(bit))
-            left.remove(bit)
-            part = add(mine, swap(other, devices, 1 << bit))
-        done.append(part[0])
-    return jnp.concatenate(done, axis=1)
+    return [total[:, :, :wide], total[:, :, wide:]]
+
+
+def project_rest(parts, devices, me):
+    while parts[0].shape[0] > 1:
+        parts = project_next(parts, devices, me)
+    return jnp.concatenate([p[0] for p in parts], axis=1)
 
 
 def on_device(
@@ -285,46 +308,91 @@
     source = my_slots // count
     lengths = lax.dynamic_slice_in_dim(cached_len, owner_id * count, count)
 
-    def exchange(x):
-        return lax.all_to_all(x, "cache", split_axis=0, concat_axis=0, tiled=True)
-
-    def pick(x):
-        return jnp.concatenate([lax.dynamic_slice_in_dim(x, picked_slot[o], 1, 0) for o in range(owners)], axis=0)
-
-    start = exchange(pick(kept_state).astype(bf16))
-    landed = exchange(pick(kept_kv.transpose(0, 2, 1, 3)))
+    places = source ^ owner_id
+
+    def send_on(x, distance):
+        block = lax.dynamic_slice_in_dim(x, picked_slot[owner_id ^ distance], 1, 0)
+        return swap(block, owners, distance, "cache") if distance else block
+
+    state_bf16 = kept_state.astype(bf16)
+    start = jnp.concatenate([send_on(state_bf16, r) for r in range(owners)], axis=0)
 
     heads_dev = query_cols // HD
     kv_head = me * heads_dev // (AH // KVH)
     fresh_all = lax.all_gather(fresh_kv.transpose(2, 0, 1, 3), "head", axis=0, tiled=False)
 
-    own = lax.dynamic_slice_in_dim(landed, kv_head * HD, HD, 3)
-    other = lax.dynamic_slice_in_dim(landed, (1 - kv_head) * HD, HD, 3)
     half = devices // 2
-    near = jnp.stack([own, swap(other, devices, half)])
+    own = lax.dynamic_slice_in_dim(kept_kv, kv_head * HD, HD, 3).transpose(0, 2, 1, 3)
+    other = lax.dynamic_slice_in_dim(kept_kv, (1 - kv_head) * HD, HD, 3).transpose(0, 2, 1, 3)
+    both = jnp.stack([own, swap(other, devices, half)], axis=1)
+    blocks = [send_on(both, r) for r in range(owners)]
+
+    calls = count // PAIR * PARTS
     bit = half // 2
+    crossed = [swap(block, devices, bit) for block in blocks]
+    needed = [[] for _ in range(calls - 1)]
+    for r in range(1, owners):
+        arrival = min((r - 1) * (calls - 1) // (owners - 1), calls - 2)
+        needed[arrival].append(blocks[r])
+        if arrival + 1 < calls - 1:
+            needed[arrival + 1].append(crossed[r])
+    needed[min(1, calls - 2)].append(crossed[0])
+    needed[-1].append(fresh_all)
+
+    running, columns = block_rates(write_strength, decay_log)
+    heads, states, call = None, [], 0
+    for pair in range(count // PAIR):
+        begin, index = start, lax.slice_in_dim(places, pair * PAIR, (pair + 1) * PAIR)
+        for part in range(PARTS):
+            deps = needed[call - 1] if call else []
+            heads, begin = delta_part(
+                delta_query,
+                delta_key,
+                delta_value,
+                delta_gate,
+                running,
+                columns,
+                begin,
+                index,
+                heads,
+                pair,
+                part,
+                deps,
+            )
+            index = jnp.arange(PAIR, dtype=jnp.int32)
+            call += 1
+        states.append(begin)
+    final_state = jnp.concatenate(states, axis=0)
+
+    near = [jnp.stack([x[0] for x in side], axis=1) for side in (blocks, crossed)]
+    near = jnp.concatenate(near, axis=0)
+    bit //= 2
     while bit > 1:
         near = jnp.concatenate([near, swap(near, devices, bit)], axis=0)
         bit //= 2
     far = swap(near, devices, 1)
 
-    delta_heads, final_state = delta_layer(
-        delta_query, delta_key, delta_value, delta_gate, write_strength, decay_log, start, source
-    )
     block_rows = count * fresh_len // devices
-    delta_mixed = project(delta_heads.reshape(devices, block_rows, -1), delta_out_weight, devices, me)
-
+    total = project_first(heads.reshape(devices, block_rows, -1), delta_out_weight, devices, me)
     scalars = jnp.stack([kv_head, me]).astype(jnp.int32)
     q4 = attn_query.reshape(count, fresh_len // block_rows, block_rows, query_cols)
     gate4 = attn_gate.reshape(q4.shape)
+    parts = column_halves(total)
+    deps = [total]
     done = []
     for chunk in range(CHUNKS):
-        heads = attend(
-            chunk, block_rows, devices, q4, gate4, near, far, fresh_all, scalars, lengths, source
+        mixed = attend(
+            chunk, block_rows, devices, q4, gate4, near, far, fresh_all, scalars, lengths, places, deps
         )
-        heads = heads.reshape(devices, block_rows // CHUNKS, query_cols)
-        done.append(project(heads, attn_out_weight, devices, me))
-    return (delta_mixed, jnp.concatenate(done, axis=0), final_state)
+        mixed = mixed.reshape(devices, block_rows // CHUNKS, query_cols)
+        total = project_first(mixed, attn_out_weight, devices, me)
+        if parts[0].shape[0] > 1:
+            parts = project_next(parts, devices, me)
+        deps = [total, *parts]
+        done.append(total)
+    delta_mixed = project_rest(parts, devices, me)
+    attn_mixed = [project_rest(column_halves(total), devices, me) for total in done]
+    return (delta_mixed, jnp.concatenate(attn_mixed, axis=0), final_state)
 
 
 def solution(mesh):

time: 278 us -> 267 us (0.960); the launches traced: 277 us -> 263 us
  waiting for transfers between devices: 113 us -> 71.7 us
  local copies, waits for them, and re-layouts: 21.4 us -> 40.6 us
  starting transfers between devices: 26.3 us -> 30.5 us
    all_to_all x2 -> x0, waiting for transfers between devices: 35.3 us -> none  [exchange(): return lax.all_to_all(x, 'cache', split_axis=0, concat_axis=0, tiled=True)]
    unnamed x37 -> x93, local copies, waits for them, and re-layouts: 11.6 us -> 30 us
    ppermute x18 -> x27, starting transfers between devices: 15.6 us -> 30.4 us  [swap(): return lax.ppermute(x, axis, [(h, h ^ bit) for h in range(devices)])]
    all_to_all x2 -> x0, starting transfers between devices: 10.7 us -> none  [exchange(): return lax.all_to_all(x, 'cache', split_axis=0, concat_axis=0, tiled=True)]
    ppermute x18 -> x27, waiting for transfers between devices: 77.7 us -> 71.7 us  [swap(): return lax.ppermute(x, axis, [(h, h ^ bit) for h in range(devices)])]
    convert_element_type x9, other arithmetic: 10.1 us -> 15.1 us  [add(): return (a.astype(f32) + b.astype(f32)).astype(bf16)]
    another operation x2 -> x1, other arithmetic: 5.89 us -> 1.37 us  [on_device(): both = jnp.stack([own, swap(other, devices, half)], axis=1)]
    dynamic_slice x0 -> x3, local copies, waits for them, and re-layouts: none -> 4.07 us  [the longest x1 2.71 us: on_device(): lax.dynamic_slice_in_dim(kept_kv, (1 - kv_head) * HD, HD, 3)]
  transfers between devices with their start and end apart: 21 -> 28, of which waited for: 13 -> 11; matrix products, arithmetic and copies ran while one was open for 13% -> 17% of each run, Pallas kernels for 4% -> 14%
where the time goes in v1:
time: 267 us; the launch traced here: 263 us
  waiting for transfers between devices  71.7 us (27%)
  Pallas kernels  56.9 us (21%)
  local copies, waits for them, and re-layouts  40.6 us (15%)
  starting transfers between devices  30.5 us (11%)
  other arithmetic  25.8 us (10%)
  between operations  22.5 us (8%)
  matrix products  15.4 us (6%)
    ppermute x27, waiting for transfers between devices, swap(): return lax.ppermute(x, axis, [(h, h ^ bit) for h in range(devices)])  71.7 us
    pallas_call x4, Pallas kernels, delta_part(): pl.pallas_call(functools.partial(delta_kernel, len(unread)), grid_spec=pl...  36.7 us
    ppermute x27, starting transfers between devices, swap(): return lax.ppermute(x, axis, [(h, h ^ bit) for h in range(devices)])  30.4 us
    unnamed x93, local copies, waits for them, and re-layouts  30 us
    pallas_call x2, Pallas kernels, attend(): pl.pallas_call(functools.partial(attend_kernel, chunk, block_rows, device...  20.2 us
    dot_general x6, matrix products, product(): out = jnp.dot(x.reshape(-1, x.shape[2]), weight, preferred_element_type=f32)  15.1 us
    convert_element_type x9, other arithmetic, add(): return (a.astype(f32) + b.astype(f32)).astype(bf16)  15.1 us
  transfers between devices with their start and end apart: 28, of which 11 were waited for; matrix products, arithmetic and copies ran while one was open for 17% of the time, Pallas kernels for 14%

profile of v1, /device:TPU:0, one launch (start us, length us, event | category | flops | bytes accessed | tf_op | source)
XLA Modules:
  0.0 263.2 jit_solution(15619823699495005879)
XLA Ops:
  7.2 2.0 copy.76
  16.4 1.3 convert_element_type.195
  21.0 5.1 %collective-permute-start.2 = (bf16[1,4,128,128]{3,2,1,0:T(8,128)(2,1)}, bf16[1,4,128,128]{3,2,1,0:T(8,128)(2,1)}, u32[]{:S(2)}, u32[]{:S(2)}) collective-permute-start(bf16[1,4,128,128]{3,2,1,0:T(8,128)(2,1)} %get-tuple-element.38), channel_id=1, source_target_pairs={{0,24},{8,16},{16,8},{24,0},{1,25},{9,17},{17,9},{25,1},{2,26},{10... | collective-permute-start | bytes 393224 | tf_op jit(solution)/shard_map/ppermute | solution.py:228
  26.6 2.7 %constant_dynamic-slice_fusion.12 = (bf16[4,128,2,256]{3,2,1,0:T(2,128)(2,1)S(1)}, bf16[4,128,2,256]{3,2,1,0:T(2,128)(2,1)}) fusion(bf16[4,128,2,512]{3,2,1,0:T(2,128)(2,1)} %param.22, s32[]{:T(128)S(6)} %select_n.195, s32[]{:T(128)S(6)} %select_n.194), kind=kLoop, calls=%fused_computation.82 | loop fusion | bytes 2097160 | tf_op jit(solution)/shard_map/dynamic_slice | solution.py:326
  30.2 1.7 collective-permute-start.3
  32.6 1.9 copy.75
  34.7 2.7 %collective-permute-done.1 = bf16[1,4,128,128]{3,2,1,0:T(8,128)(2,1)} collective-permute-done((bf16[1,4,128,128]{3,2,1,0:T(8,128)(2,1)}, bf16[1,4,128,128]{3,2,1,0:T(8,128)(2,1)}, u32[]{:S(2)}, u32[]{:S(2)}) %collective-permute-start.1) | collective-permute-done | bytes 131104 | tf_op jit(solution)/shard_map/ppermute | solution.py:228
  37.4 1.1 pad_maximum_fusion.3.start_ref
  38.6 14.4 %collective-permute-done.3 = bf16[4,2,128,256]{3,2,1,0:T(8,128)(2,1)} collective-permute-done((bf16[4,2,128,256]{3,2,1,0:T(8,128)(2,1)}, bf16[4,2,128,256]{3,2,1,0:T(8,128)(2,1)}, u32[]{:S(2)}, u32[]{:S(2)}) %collective-permute-start.3) | collective-permute-done | bytes 524320 | tf_op jit(solution)/shard_map/ppermute | solution.py:228
  53.0 1.4 fusion.15
  55.3 3.3 %collective-permute-start.6 = (bf16[1,2,2,128,256]{4,3,2,1,0:T(8,128)(2,1)S(1)}, bf16[1,2,2,128,256]{4,3,2,1,0:T(8,128)(2,1)S(1)}, u32[]{:S(2)}, u32[]{:S(2)}) collective-permute-start(bf16[1,2,2,128,256]{4,3,2,1,0:T(8,128)(2,1)S(1)} %get-tuple-element.33), channel_id=1, source_target_pairs={{0,16},{8,24},{16,0},{24,8},{1,17},{9,25},{17,1},{25,9},{2,18},{10... | collective-permute-start | bytes 786440 | tf_op jit(solution)/shard_map/ppermute | solution.py:228
  58.6 1.6 copy-done.21
  60.2 1.2 copy-done.28
  61.4 9.5 %delta_part.4 = (bf16[4,512,512]{2,1,0:T(8,128)(2,1)S(1)}, f32[2,4,128,128]{3,2,1,0:T(8,128)S(1)}) custom-call(s32[2]{0:T(128)S(1)} %get-tuple-element.41.source, bf16[4,512,256]{2,1,0:T(8,128)(2,1)S(1)} %copy-done.26, bf16[4,512,256]{2,1,0:T(8,128)(2,1)S(1)} %copy-done.28, bf16[4,512,512]{2,1,0:T(8,128)(2,1)S(1)} %copy-done.19, ...), custom_call_target="tpu_custom_call" | custom-call | flops 10000000000 | bytes 3000000 | tf_op jit(solution)/shard_map/delta_part/pallas_call | solution.py:112
  71.0 1.6 collective-permute-start.7
  73.3 1.3 collective-permute-start.8
  74.6 9.0 %delta_part.5 = (bf16[4,512,512]{2,1,0:T(8,128)(2,1)S(1)}, f32[2,4,128,128]{3,2,1,0:T(8,128)S(1)}) custom-call(s32[2]{0:T(128)S(1)} %iota.35.source, bf16[4,512,256]{2,1,0:T(8,128)(2,1)S(1)} %copy-done.26, bf16[4,512,256]{2,1,0:T(8,128)(2,1)S(1)} %copy-done.28, bf16[4,512,512]{2,1,0:T(8,128)(2,1)S(1)} %copy-done.19, ...), custom_call_target="tpu_custom_call", output_to_operand_aliasing={{0}: (8, {})} | custom-call | flops 10000000000 | bytes 3000000 | tf_op jit(solution)/shard_map/delta_part/pallas_call | solution.py:112
  84.5 9.0 %delta_part.6 = (bf16[4,512,512]{2,1,0:T(8,128)(2,1)S(1)}, f32[2,4,128,128]{3,2,1,0:T(8,128)S(1)}) custom-call(s32[2]{0:T(128)S(1)} %get-tuple-element.42.source, bf16[4,512,256]{2,1,0:T(8,128)(2,1)S(1)} %copy-done.26, bf16[4,512,256]{2,1,0:T(8,128)(2,1)S(1)} %copy-done.28, bf16[4,512,512]{2,1,0:T(8,128)(2,1)S(1)} %copy-done.19, ...), custom_call_target="tpu_custom_call", output_to_operand_aliasing={{0}: (8, {})} | custom-call | flops 10000000000 | bytes 3000000 | tf_op jit(solution)/shard_map/delta_part/pallas_call | solution.py:112
  93.5 1.3 copy-done.2
  97.1 1.6 copy-done.3
  98.7 0.9 copy-done.13
  99.6 0.9 copy-done.17
  100.6 2.2 copy-done.18
  102.7 1.6 copy-done.20
  104.3 1.6 copy-done.23
  105.9 1.2 copy-done.27
  107.1 1.2 copy-done.29
  108.4 1.0 copy-done.31
  109.4 9.1 %delta_part.7 = (bf16[4,512,512]{2,1,0:T(8,128)(2,1)S(1)}, f32[2,4,128,128]{3,2,1,0:T(8,128)S(1)}) custom-call(s32[2]{0:T(128)S(1)} %iota.30.source, bf16[4,512,256]{2,1,0:T(8,128)(2,1)S(1)} %copy-done.27, bf16[4,512,256]{2,1,0:T(8,128)(2,1)S(1)} %copy-done.29, bf16[4,512,512]{2,1,0:T(8,128)(2,1)S(1)} %copy-done.20, ...), custom_call_target="tpu_custom_call", output_to_operand_aliasing={{0}: (8, {})} | custom-call | flops 10000000000 | bytes 3000000 | tf_op jit(solution)/shard_map/delta_part/pallas_call | solution.py:112
  119.4 4.5 %convolution_convert_fusion = bf16[1024,2048]{1,0:T(8,128)(2,1)} fusion(bf16[1024,512]{1,0:T(8,128)(2,1)S(1)} %bitcast.155, bf16[512,2048]{1,0:T(8,128)(2,1)S(1)} %copy-done), kind=kOutput, calls=%fused_computation.6 | convolution fusion | flops 2149580800 | bytes 7340032 | tf_op jit(solution)/shard_map/dot_general | solution.py:247
  124.6 8.0 %collective-permute-done.15 = bf16[1,2,2,128,256]{4,3,2,1,0:T(8,128)(2,1)S(1)} collective-permute-done((bf16[1,2,2,128,256]{4,3,2,1,0:T(8,128)(2,1)S(1)}, bf16[1,2,2,128,256]{4,3,2,1,0:T(8,128)(2,1)S(1)}, u32[]{:S(2)}, u32[]{:S(2)}) %collective-permute-start.15) | collective-permute-done | bytes 262176 | tf_op jit(solution)/shard_map/ppermute | solution.py:228
  132.6 1.4 maximum_maximum_fusion.near_ref
  134.2 2.3 convolution_convert_fusion.1
  136.6 6.4 %fusion.refs_0_ = bf16[4,256,2048]{2,1,0:T(8,128)(2,1)} fusion(bf16[4,256,2048]{2,1,0:T(8,128)(2,1)S(1)} %bitcast.141, bf16[4,256,2048]{2,1,0:T(8,128)(2,1)} %collective-permute-done.10), kind=kLoop, calls=%fused_computation.1 | loop fusion | flops 8388608 | bytes 12582912 | tf_op jit(solution)/shard_map/convert_element_type | solution.py:243
  142.9 10.0 %attend.2 = bf16[4,2,128,512]{3,2,1,0:T(8,128)(2,1)S(1)} custom-call(s32[6]{0:T(128)S(1)} %pad_add_fusion.scalars, s32[4]{0:T(128)S(1)} %dynamic_slice.167.lengths, bf16[4,2,256,512]{3,2,1,0:T(8,128)(2,1)S(1)} %bitcast.133, bf16[4,2,256,512]{3,2,1,0:T(8,128)(2,1)S(1)} %bitcast.136, bf16[4,4,2,128,256]{4,3,2,1,0:T(8,128)(2,1)} %maximum_maximum_fusion.near_ref, ...), custom_call_target="tpu_custom_call" | custom-call | flops 10000000000 | bytes 8000000 | tf_op jit(solution)/shard_map/attend/pallas_call | solution.py:203
  154.8 2.6 %convolution_convert_fusion.4 = bf16[512,2048]{1,0:T(8,128)(2,1)} fusion(bf16[512,512]{1,0:T(8,128)(2,1)S(1)} %bitcast.160, bf16[512,2048]{1,0:T(8,128)(2,1)S(1)} %copy-done.42), kind=kOutput, calls=%fused_computation.10 | convolution fusion | flops 1074790400 | bytes 4718592 | tf_op jit(solution)/shard_map/dot_general | solution.py:247
  157.9 1.8 fusion.28
  159.7 1.4 copy-done.35
  161.2 2.5 collective-permute-start.13
  163.8 2.3 dynamic-slice_bitcast_fusion.1
  166.7 3.2 %convolution_convert_fusion.5 = bf16[512,2048]{1,0:T(8,128)(2,1)S(1)} fusion(bf16[512,512]{1,0:T(8,128)(2,1)} %bitcast.157, bf16[512,2048]{1,0:T(8,128)(2,1)} %param.29), kind=kOutput, calls=%fused_computation.11 | convolution fusion | flops 1074790400 | bytes 4718592 | tf_op jit(solution)/shard_map/dot_general | solution.py:247
  169.9 17.3 %collective-permute-done.13 = bf16[2,256,1024]{2,1,0:T(8,128)(2,1)} collective-permute-done((bf16[2,256,1024]{2,1,0:T(8,128)(2,1)S(1)}, bf16[2,256,1024]{2,1,0:T(8,128)(2,1)}, u32[]{:S(2)}, u32[]{:S(2)}) %collective-permute-start.13) | collective-permute-done | bytes 1048608 | tf_op jit(solution)/shard_map/ppermute | solution.py:228
  187.2 1.6 fusion.3.refs_2_
  189.7 1.5 collective-permute-done.11
  191.1 1.6 fusion.4.refs_1_
  193.2 3.9 %fusion.2.refs_0_ = bf16[4,128,2048]{2,1,0:T(8,128)(2,1)} fusion(bf16[4,128,2048]{2,1,0:T(8,128)(2,1)S(1)} %bitcast.150, bf16[4,128,2048]{2,1,0:T(8,128)(2,1)} %collective-permute-done.17), kind=kLoop, calls=%fused_computation.5 | loop fusion | flops 4194304 | bytes 6291456 | tf_op jit(solution)/shard_map/convert_element_type | solution.py:243
  197.1 10.2 %attend.3 = bf16[4,2,128,512]{3,2,1,0:T(8,128)(2,1)S(1)} custom-call(s32[6]{0:T(128)S(1)} %pad_add_fusion.scalars, s32[4]{0:T(128)S(1)} %dynamic_slice.167.lengths, bf16[4,2,256,512]{3,2,1,0:T(8,128)(2,1)S(1)} %bitcast.134, bf16[4,2,256,512]{3,2,1,0:T(8,128)(2,1)} %bitcast.135, bf16[4,4,2,128,256]{4,3,2,1,0:T(8,128)(2,1)} %maximum_maximum_fusion.near_ref, ...), custom_call_target="tpu_custom_call" | custom-call | flops 10000000000 | bytes 8000000 | tf_op jit(solution)/shard_map/attend/pallas_call | solution.py:203
  207.4 1.5 copy-done.43
  208.9 1.3 convolution_convert_fusion.2
  210.2 1.0 pad_maximum_fusion.2
  211.7 1.2 copy-done.33
  213.1 1.8 collective-permute-start.20
  214.8 1.0 pad_maximum_fusion
  216.7 1.3 convolution_convert_fusion.3
  218.0 9.5 %collective-permute-done.20 = bf16[2,128,1024]{2,1,0:T(8,128)(2,1)S(1)} collective-permute-done((bf16[2,128,1024]{2,1,0:T(8,128)(2,1)S(1)}, bf16[2,128,1024]{2,1,0:T(8,128)(2,1)S(1)}, u32[]{:S(2)}, u32[]{:S(2)}) %collective-permute-start.20) | collective-permute-done | bytes 524320 | tf_op jit(solution)/shard_map/ppermute | solution.py:228
  227.7 1.3 collective-permute-start.21
  230.1 1.2 collective-permute-start.25
  233.4 3.6 %collective-permute-done.21 = bf16[1,128,1024]{2,1,0:T(8,128)(2,1)S(1)} collective-permute-done((bf16[1,128,1024]{2,1,0:T(8,128)(2,1)S(1)}, bf16[1,128,1024]{2,1,0:T(8,128)(2,1)S(1)}, u32[]{:S(2)}, u32[]{:S(2)}) %collective-permute-start.21) | collective-permute-done | bytes 262176 | tf_op jit(solution)/shard_map/ppermute | solution.py:228
  237.1 8.0 %collective-permute-done.25 = bf16[2,128,1024]{2,1,0:T(8,128)(2,1)S(1)} collective-permute-done((bf16[2,128,1024]{2,1,0:T(8,128)(2,1)S(1)}, bf16[2,128,1024]{2,1,0:T(8,128)(2,1)S(1)}, u32[]{:S(2)}, u32[]{:S(2)}) %collective-permute-start.25) | collective-permute-done | bytes 524320 | tf_op jit(solution)/shard_map/ppermute | solution.py:228
  246.1 2.1 collective-permute-done.23
  248.5 1.8 collective-permute-start.24
  250.3 2.2 collective-permute-done.26
  252.6 2.3 collective-permute-done.24
  255.0 1.1 maximum_maximum_fusion.1
  (156 shorter events, 22.4 us)
Async XLA Ops:
  7.2 112.2 %copy-start = (bf16[512,2048]{1,0:T(8,128)(2,1)S(1)}, bf16[512,2048]{1,0:T(8,128)(2,1)}, u32[]{:S(2)}) copy-start(bf16[512,2048]{1,0:T(8,128)(2,1)} %param.28) | copy-start | bytes 6291460
  7.2 89.9 %all-gather.3.cloned.1.call-start = ((), (), s32[]{:S(2)}) async-start(), calls=%async_computation | async-start | bytes 4718592 | tf_op jit(solution)/shard_map/all_gather | solution.py:322
  20.2 11.7 %copy-start.39 = (f32[4,4,512]{2,1,0:T(4,128)S(1)}, f32[4,4,512]{2,1,0:T(4,128)}, u32[]{:S(2)}) copy-start(f32[4,4,512]{2,1,0:T(4,128)} %param.20) | copy-start | bytes 98308
  20.2 12.0 %copy-start.40 = (f32[4,4,512]{2,1,0:T(4,128)S(1)}, f32[4,4,512]{2,1,0:T(4,128)}, u32[]{:S(2)}) copy-start(f32[4,4,512]{2,1,0:T(4,128)} %param.19) | copy-start | bytes 98308
  21.0 13.7 %collective-permute-start.2 = (bf16[1,4,128,128]{3,2,1,0:T(8,128)(2,1)}, bf16[1,4,128,128]{3,2,1,0:T(8,128)(2,1)}, u32[]{:S(2)}, u32[]{:S(2)}) collective-permute-start(bf16[1,4,128,128]{3,2,1,0:T(8,128)(2,1)} %get-tuple-element.38), channel_id=1, source_target_pairs={{0,24},{8,16},{16,8},{24,0},{1,25},{9,17},{17,9},{25,1},{2,26},{10... | collective-permute-start | bytes 393224 | tf_op jit(solution)/shard_map/ppermute | solution.py:228
  26.1 11.4 %collective-permute-start.1 = (bf16[1,4,128,128]{3,2,1,0:T(8,128)(2,1)}, bf16[1,4,128,128]{3,2,1,0:T(8,128)(2,1)}, u32[]{:S(2)}, u32[]{:S(2)}) collective-permute-start(bf16[1,4,128,128]{3,2,1,0:T(8,128)(2,1)} %get-tuple-element.39), channel_id=1, source_target_pairs={{0,16},{8,24},{16,0},{24,8},{1,17},{9,25},{17,1},{25,9},{2,18},{10... | collective-permute-start | bytes 393224 | tf_op jit(solution)/shard_map/ppermute | solution.py:228
  26.1 11.4 %collective-permute-start = (bf16[1,4,128,128]{3,2,1,0:T(8,128)(2,1)S(1)}, bf16[1,4,128,128]{3,2,1,0:T(8,128)(2,1)}, u32[]{:S(2)}, u32[]{:S(2)}) collective-permute-start(bf16[1,4,128,128]{3,2,1,0:T(8,128)(2,1)S(1)} %get-tuple-element.40), channel_id=1, source_target_pairs={{0,8},{8,0},{16,24},{24,16},{1,9},{9,1},{17,25},{25,17},{2,10},{10... | collective-permute-start | bytes 393224 | tf_op jit(solution)/shard_map/ppermute | solution.py:228
  29.3 5.2 %copy-start.41 = (s32[16]{0:T(128)S(1)}, s32[16]{0:T(128)}, u32[]{:S(2)}) copy-start(s32[16]{0:T(128)} %param.27) | copy-start | bytes 196
  30.2 22.8 %collective-permute-start.3 = (bf16[4,2,128,256]{3,2,1,0:T(8,128)(2,1)}, bf16[4,2,128,256]{3,2,1,0:T(8,128)(2,1)}, u32[]{:S(2)}, u32[]{:S(2)}) collective-permute-start(bf16[4,2,128,256]{3,2,1,0:T(8,128)(2,1)} %bitcast.116), channel_id=1, source_target_pairs={{0,4},{1,5},{2,6},{3,7},{4,0},{5,1},{6,2},{7,3},{8,12},{9,13},{10,... | collective-permute-start | bytes 1572872 | tf_op jit(solution)/shard_map/ppermute | solution.py:228
  34.5 24.1 %copy-start.19 = (bf16[4,512,512]{2,1,0:T(8,128)(2,1)S(1)}, bf16[4,512,512]{2,1,0:T(8,128)(2,1)}, u32[]{:S(2)}) copy-start(bf16[4,512,512]{2,1,0:T(8,128)(2,1)} %v_ref.7) | copy-start | bytes 6291460
  34.5 24.1 %copy-start.26 = (bf16[4,512,256]{2,1,0:T(8,128)(2,1)S(1)}, bf16[4,512,256]{2,1,0:T(8,128)(2,1)}, u32[]{:S(2)}) copy-start(bf16[4,512,256]{2,1,0:T(8,128)(2,1)} %q_ref.7) | copy-start | bytes 3145732
  54.4 16.6 %copy-start.37 = (bf16[1,2,2,128,256]{4,3,2,1,0:T(8,128)(2,1)}, bf16[1,2,2,128,256]{4,3,2,1,0:T(8,128)(2,1)S(1)}, u32[]{:S(2)}) copy-start(bf16[1,2,2,128,256]{4,3,2,1,0:T(8,128)(2,1)S(1)} %get-tuple-element.34) | copy-start | bytes 786436
  54.4 18.2 %collective-permute-start.4 = (bf16[1,2,2,128,256]{4,3,2,1,0:T(8,128)(2,1)S(1)}, bf16[1,2,2,128,256]{4,3,2,1,0:T(8,128)(2,1)S(1)}, u32[]{:S(2)}, u32[]{:S(2)}) collective-permute-start(bf16[1,2,2,128,256]{4,3,2,1,0:T(8,128)(2,1)S(1)} %get-tuple-element.32), channel_id=1, source_target_pairs={{0,8},{8,0},{16,24},{24,16},{1,9},{9,1},{17,25},{25,17},{2,10},{10... | collective-permute-start | bytes 786440 | tf_op jit(solution)/shard_map/ppermute | solution.py:228
  55.3 18.0 %collective-permute-start.6 = (bf16[1,2,2,128,256]{4,3,2,1,0:T(8,128)(2,1)S(1)}, bf16[1,2,2,128,256]{4,3,2,1,0:T(8,128)(2,1)S(1)}, u32[]{:S(2)}, u32[]{:S(2)}) collective-permute-start(bf16[1,2,2,128,256]{4,3,2,1,0:T(8,128)(2,1)S(1)} %get-tuple-element.33), channel_id=1, source_target_pairs={{0,16},{8,24},{16,0},{24,8},{1,17},{9,25},{17,1},{25,9},{2,18},{10... | collective-permute-start | bytes 786440 | tf_op jit(solution)/shard_map/ppermute | solution.py:228
  58.6 1.6 copy-start.21
  60.2 1.2 copy-start.28
  61.4 13.2 %copy-start.22 = (bf16[4,512,512]{2,1,0:T(8,128)(2,1)S(1)}, bf16[4,512,512]{2,1,0:T(8,128)(2,1)}, u32[]{:S(2)}) copy-start(bf16[4,512,512]{2,1,0:T(8,128)(2,1)} %gate_ref.7) | copy-start | bytes 6291460
  71.0 13.4 %collective-permute-start.7 = (bf16[1,2,2,128,256]{4,3,2,1,0:T(8,128)(2,1)S(1)}, bf16[1,2,2,128,256]{4,3,2,1,0:T(8,128)(2,1)S(1)}, u32[]{:S(2)}, u32[]{:S(2)}) collective-permute-start(bf16[1,2,2,128,256]{4,3,2,1,0:T(8,128)(2,1)S(1)} %get-tuple-element.34), channel_id=1, source_target_pairs={{0,2},{1,3},{2,0},{3,1},{4,6},{5,7},{6,4},{7,5},{8,10},{9,11},{10,... | collective-permute-start | bytes 786440 | tf_op jit(solution)/shard_map/ppermute | solution.py:228
  72.6 23.0 %collective-permute-start.9 = (bf16[1,2,2,128,256]{4,3,2,1,0:T(8,128)(2,1)S(1)}, bf16[1,2,2,128,256]{4,3,2,1,0:T(8,128)(2,1)S(1)}, u32[]{:S(2)}, u32[]{:S(2)}) collective-permute-start(bf16[1,2,2,128,256]{4,3,2,1,0:T(8,128)(2,1)S(1)} %get-tuple-element.31), channel_id=1, source_target_pairs={{0,24},{8,16},{16,8},{24,0},{1,25},{9,17},{17,9},{25,1},{2,26},{10... | collective-permute-start | bytes 786440 | tf_op jit(solution)/shard_map/ppermute | solution.py:228
  72.6 11.8 %collective-permute-start.5 = (bf16[1,2,2,128,256]{4,3,2,1,0:T(8,128)(2,1)S(1)}, bf16[1,2,2,128,256]{4,3,2,1,0:T(8,128)(2,1)S(1)}, u32[]{:S(2)}, u32[]{:S(2)}) collective-permute-start(bf16[1,2,2,128,256]{4,3,2,1,0:T(8,128)(2,1)S(1)} %collective-permute-done.4.refs_1_), channel_id=1, source_target_pairs={{0,2},{1,3},{2,0},{3,1},{4,6},{5,7},{6,4},{7,5},{8,10},{9,11},{10,... | collective-permute-start | bytes 786440 | tf_op jit(solution)/shard_map/ppermute | solution.py:228
  73.3 11.1 %copy-start.8 = (bf16[1,2,2,128,256]{4,3,2,1,0:T(8,128)(2,1)}, bf16[1,2,2,128,256]{4,3,2,1,0:T(8,128)(2,1)S(1)}, u32[]{:S(2)}) copy-start(bf16[1,2,2,128,256]{4,3,2,1,0:T(8,128)(2,1)S(1)} %collective-permute-done.6.refs_2_) | copy-start | bytes 786436
  73.3 23.0 %collective-permute-start.8 = (bf16[1,2,2,128,256]{4,3,2,1,0:T(8,128)(2,1)S(1)}, bf16[1,2,2,128,256]{4,3,2,1,0:T(8,128)(2,1)S(1)}, u32[]{:S(2)}, u32[]{:S(2)}) collective-permute-start(bf16[1,2,2,128,256]{4,3,2,1,0:T(8,128)(2,1)S(1)} %collective-permute-done.6.refs_2_), channel_id=1, source_target_pairs={{0,2},{1,3},{2,0},{3,1},{4,6},{5,7},{6,4},{7,5},{8,10},{9,11},{10,... | collective-permute-start | bytes 786440 | tf_op jit(solution)/shard_map/ppermute | solution.py:228
  84.4 9.1 %copy-start.10 = (bf16[1,2,2,128,256]{4,3,2,1,0:T(8,128)(2,1)}, bf16[1,2,2,128,256]{4,3,2,1,0:T(8,128)(2,1)S(1)}, u32[]{:S(2)}) copy-start(bf16[1,2,2,128,256]{4,3,2,1,0:T(8,128)(2,1)S(1)} %collective-permute-done.7.refs_3_) | copy-start | bytes 786436
  84.4 9.1 %copy-start.14 = (bf16[1,2,2,128,256]{4,3,2,1,0:T(8,128)(2,1)}, bf16[1,2,2,128,256]{4,3,2,1,0:T(8,128)(2,1)S(1)}, u32[]{:S(2)}) copy-start(bf16[1,2,2,128,256]{4,3,2,1,0:T(8,128)(2,1)S(1)} %collective-permute-done.5.refs_1_) | copy-start | bytes 786436
  93.5 1.3 copy-start.2
  97.1 1.6 copy-start.3
  100.5 2.2 copy-start.18
  102.7 1.6 copy-start.20
  104.3 1.6 copy-start.23
  107.1 1.2 copy-start.29
  119.4 13.2 %copy-start.9 = (bf16[1,2,2,128,256]{4,3,2,1,0:T(8,128)(2,1)S(1)}, bf16[1,2,2,128,256]{4,3,2,1,0:T(8,128)(2,1)}, u32[]{:S(2)}) copy-start(bf16[1,2,2,128,256]{4,3,2,1,0:T(8,128)(2,1)} %copy-done.8) | copy-start | bytes 786436
  119.4 13.2 %copy-start.11 = (bf16[1,2,2,128,256]{4,3,2,1,0:T(8,128)(2,1)S(1)}, bf16[1,2,2,128,256]{4,3,2,1,0:T(8,128)(2,1)}, u32[]{:S(2)}) copy-start(bf16[1,2,2,128,256]{4,3,2,1,0:T(8,128)(2,1)} %copy-done.10) | copy-start | bytes 786436
  119.4 13.2 %copy-start.15 = (bf16[1,2,2,128,256]{4,3,2,1,0:T(8,128)(2,1)S(1)}, bf16[1,2,2,128,256]{4,3,2,1,0:T(8,128)(2,1)}, u32[]{:S(2)}) copy-start(bf16[1,2,2,128,256]{4,3,2,1,0:T(8,128)(2,1)} %copy-done.14) | copy-start | bytes 786436
  119.4 13.2 %copy-start.38 = (bf16[1,2,2,128,256]{4,3,2,1,0:T(8,128)(2,1)S(1)}, bf16[1,2,2,128,256]{4,3,2,1,0:T(8,128)(2,1)}, u32[]{:S(2)}) copy-start(bf16[1,2,2,128,256]{4,3,2,1,0:T(8,128)(2,1)} %copy-done.37) | copy-start | bytes 786436
  123.8 12.7 %collective-permute-start.10 = (bf16[4,256,2048]{2,1,0:T(8,128)(2,1)}, bf16[4,256,2048]{2,1,0:T(8,128)(2,1)}, u32[]{:S(2)}, u32[]{:S(2)}) collective-permute-start(bf16[4,256,2048]{2,1,0:T(8,128)(2,1)} %bitcast.16), channel_id=1, source_target_pairs={{0,1},{1,0},{2,3},{3,2},{4,5},{5,4},{6,7},{7,6},{8,9},{9,8},{10,11... | collective-permute-start | bytes 12582920 | tf_op jit(solution)/shard_map/ppermute | solution.py:228
  123.8 8.7 %collective-permute-start.15 = (bf16[1,2,2,128,256]{4,3,2,1,0:T(8,128)(2,1)S(1)}, bf16[1,2,2,128,256]{4,3,2,1,0:T(8,128)(2,1)S(1)}, u32[]{:S(2)}, u32[]{:S(2)}) collective-permute-start(bf16[1,2,2,128,256]{4,3,2,1,0:T(8,128)(2,1)S(1)} %copy-done.13), channel_id=1, source_target_pairs={{0,2},{1,3},{2,0},{3,1},{4,6},{5,7},{6,4},{7,5},{8,10},{9,11},{10,... | collective-permute-start | bytes 786440 | tf_op jit(solution)/shard_map/ppermute | solution.py:228
  132.6 1.5 copy-start.44
  134.0 8.9 %collective-permute-start.16 = (bf16[4,4,2,128,256]{4,3,2,1,0:T(8,128)(2,1)}, bf16[4,4,2,128,256]{4,3,2,1,0:T(8,128)(2,1)}, u32[]{:S(2)}, u32[]{:S(2)}) collective-permute-start(bf16[4,4,2,128,256]{4,3,2,1,0:T(8,128)(2,1)} %maximum_maximum_fusion.near_ref), channel_id=1, source_target_pairs={{0,1},{1,0},{2,3},{3,2},{4,5},{5,4},{6,7},{7,6},{8,9},{9,8},{10,11... | collective-permute-start | bytes 6291464 | tf_op jit(solution)/shard_map/ppermute | solution.py:228
  136.5 6.4 %copy-start.24 = (bf16[4,512,512]{2,1,0:T(8,128)(2,1)S(1)}, bf16[4,512,512]{2,1,0:T(8,128)(2,1)}, u32[]{:S(2)}) copy-start(bf16[4,512,512]{2,1,0:T(8,128)(2,1)} %param.24) | copy-start | bytes 6291460
  136.6 6.4 %copy-start.25 = (bf16[4,512,512]{2,1,0:T(8,128)(2,1)S(1)}, bf16[4,512,512]{2,1,0:T(8,128)(2,1)}, u32[]{:S(2)}) copy-start(bf16[4,512,512]{2,1,0:T(8,128)(2,1)} %param.25) | copy-start | bytes 6291460
  153.0 1.8 copy-start.42
  154.8 3.2 %copy-start.32 = (bf16[4,256,2048]{2,1,0:T(8,128)(2,1)S(1)}, bf16[4,256,2048]{2,1,0:T(8,128)(2,1)}, u32[]{:S(2)}) copy-start(bf16[4,256,2048]{2,1,0:T(8,128)(2,1)} %fusion.refs_0_) | copy-start | bytes 12582916
  157.4 35.8 %collective-permute-start.17 = (bf16[4,128,2048]{2,1,0:T(8,128)(2,1)}, bf16[4,128,2048]{2,1,0:T(8,128)(2,1)}, u32[]{:S(2)}, u32[]{:S(2)}) collective-permute-start(bf16[4,128,2048]{2,1,0:T(8,128)(2,1)} %bitcast.43), channel_id=1, source_target_pairs={{0,1},{1,0},{2,3},{3,2},{4,5},{5,4},{6,7},{7,6},{8,9},{9,8},{10,11... | collective-permute-start | bytes 6291464 | tf_op jit(solution)/shard_map/ppermute | solution.py:228
  159.7 1.4 copy-start.35
  161.2 26.0 %collective-permute-start.13 = (bf16[2,256,1024]{2,1,0:T(8,128)(2,1)S(1)}, bf16[2,256,1024]{2,1,0:T(8,128)(2,1)}, u32[]{:S(2)}, u32[]{:S(2)}) collective-permute-start(bf16[2,256,1024]{2,1,0:T(8,128)(2,1)S(1)} %dynamic-slice_bitcast_fusion), channel_id=1, source_target_pairs={{0,4},{1,5},{2,6},{3,7},{4,0},{5,1},{6,2},{7,3},{8,12},{9,13},{10,... | collective-permute-start | bytes 3145736 | tf_op jit(solution)/shard_map/ppermute | solution.py:228
  166.0 25.1 %collective-permute-start.11 = (bf16[2,256,1024]{2,1,0:T(8,128)(2,1)}, bf16[2,256,1024]{2,1,0:T(8,128)(2,1)}, u32[]{:S(2)}, u32[]{:S(2)}) collective-permute-start(bf16[2,256,1024]{2,1,0:T(8,128)(2,1)} %dynamic-slice_bitcast_fusion.1), channel_id=1, source_target_pairs={{0,2},{1,3},{2,0},{3,1},{4,6},{5,7},{6,4},{7,5},{8,10},{9,11},{10,... | collective-permute-start | bytes 3145736 | tf_op jit(solution)/shard_map/ppermute | solution.py:228
  166.7 20.5 %copy-start.36 = (bf16[4,256,1024]{2,1,0:T(8,128)(2,1)S(1)}, bf16[4,256,1024]{2,1,0:T(8,128)(2,1)}, u32[]{:S(2)}) copy-start(bf16[4,256,1024]{2,1,0:T(8,128)(2,1)} %copy-done.35) | copy-start | bytes 6291460
  169.9 21.2 %copy-start.34 = (bf16[4,256,1024]{2,1,0:T(8,128)(2,1)S(1)}, bf16[4,256,1024]{2,1,0:T(8,128)(2,1)}, u32[]{:S(2)}) copy-start(bf16[4,256,1024]{2,1,0:T(8,128)(2,1)} %get-tuple-element.19) | copy-start | bytes 6291460
  188.9 22.4 %collective-permute-start.14 = (bf16[1,256,1024]{2,1,0:T(8,128)(2,1)S(1)}, bf16[1,256,1024]{2,1,0:T(8,128)(2,1)S(1)}, u32[]{:S(2)}, u32[]{:S(2)}) collective-permute-start(bf16[1,256,1024]{2,1,0:T(8,128)(2,1)S(1)} %constant_dynamic-slice_fusion.8), channel_id=1, source_target_pairs={{0,2},{1,3},{2,0},{3,1},{4,6},{5,7},{6,4},{7,5},{8,10},{9,11},{10,... | collective-permute-start | bytes 1572872 | tf_op jit(solution)/shard_map/ppermute | solution.py:228
  192.8 18.7 %collective-permute-start.12 = (bf16[1,256,1024]{2,1,0:T(8,128)(2,1)S(1)}, bf16[1,256,1024]{2,1,0:T(8,128)(2,1)S(1)}, u32[]{:S(2)}, u32[]{:S(2)}) collective-permute-start(bf16[1,256,1024]{2,1,0:T(8,128)(2,1)S(1)} %constant_dynamic-slice_fusion.9), channel_id=1, source_target_pairs={{0,4},{1,5},{2,6},{3,7},{4,0},{5,1},{6,2},{7,3},{8,12},{9,13},{10,... | collective-permute-start | bytes 1572872 | tf_op jit(solution)/shard_map/ppermute | solution.py:228
  207.3 1.6 copy-start.43
  208.9 1.3 copy-start.5
  208.9 1.4 copy-start.7
  210.1 18.9 %collective-permute-start.22 = (bf16[4,128,2048]{2,1,0:T(8,128)(2,1)S(1)}, bf16[4,128,2048]{2,1,0:T(8,128)(2,1)S(1)}, u32[]{:S(2)}, u32[]{:S(2)}) collective-permute-start(bf16[4,128,2048]{2,1,0:T(8,128)(2,1)S(1)} %bitcast.162), channel_id=1, source_target_pairs={{0,1},{1,0},{2,3},{3,2},{4,5},{5,4},{6,7},{7,6},{8,9},{9,8},{10,11... | collective-permute-start | bytes 6291464 | tf_op jit(solution)/shard_map/ppermute | solution.py:228
  211.3 1.6 copy-start.33
  213.1 14.4 %collective-permute-start.20 = (bf16[2,128,1024]{2,1,0:T(8,128)(2,1)S(1)}, bf16[2,128,1024]{2,1,0:T(8,128)(2,1)S(1)}, u32[]{:S(2)}, u32[]{:S(2)}) collective-permute-start(bf16[2,128,1024]{2,1,0:T(8,128)(2,1)S(1)} %dynamic-slice_bitcast_fusion.4), channel_id=1, source_target_pairs={{0,4},{1,5},{2,6},{3,7},{4,0},{5,1},{6,2},{7,3},{8,12},{9,13},{10,... | collective-permute-start | bytes 1572872 | tf_op jit(solution)/shard_map/ppermute | solution.py:228
  215.9 15.4 %collective-permute-start.18 = (bf16[2,128,1024]{2,1,0:T(8,128)(2,1)S(1)}, bf16[2,128,1024]{2,1,0:T(8,128)(2,1)S(1)}, u32[]{:S(2)}, u32[]{:S(2)}) collective-permute-start(bf16[2,128,1024]{2,1,0:T(8,128)(2,1)S(1)} %dynamic-slice_bitcast_fusion.5), channel_id=1, source_target_pairs={{0,2},{1,3},{2,0},{3,1},{4,6},{5,7},{6,4},{7,5},{8,10},{9,11},{10,... | collective-permute-start | bytes 1572872 | tf_op jit(solution)/shard_map/ppermute | solution.py:228
  227.7 9.3 %collective-permute-start.21 = (bf16[1,128,1024]{2,1,0:T(8,128)(2,1)S(1)}, bf16[1,128,1024]{2,1,0:T(8,128)(2,1)S(1)}, u32[]{:S(2)}, u32[]{:S(2)}) collective-permute-start(bf16[1,128,1024]{2,1,0:T(8,128)(2,1)S(1)} %constant_dynamic-slice_fusion.4), channel_id=1, source_target_pairs={{0,2},{1,3},{2,0},{3,1},{4,6},{5,7},{6,4},{7,5},{8,10},{9,11},{10,... | collective-permute-start | bytes 786440 | tf_op jit(solution)/shard_map/ppermute | solution.py:228
  230.1 14.9 %collective-permute-start.25 = (bf16[2,128,1024]{2,1,0:T(8,128)(2,1)S(1)}, bf16[2,128,1024]{2,1,0:T(8,128)(2,1)S(1)}, u32[]{:S(2)}, u32[]{:S(2)}) collective-permute-start(bf16[2,128,1024]{2,1,0:T(8,128)(2,1)S(1)} %dynamic-slice_bitcast_fusion.2), channel_id=1, source_target_pairs={{0,4},{1,5},{2,6},{3,7},{4,0},{5,1},{6,2},{7,3},{8,12},{9,13},{10,... | collective-permute-start | bytes 1572872 | tf_op jit(solution)/shard_map/ppermute | solution.py:228
  231.6 18.7 %collective-permute-start.19 = (bf16[1,128,1024]{2,1,0:T(8,128)(2,1)S(1)}, bf16[1,128,1024]{2,1,0:T(8,128)(2,1)S(1)}, u32[]{:S(2)}, u32[]{:S(2)}) collective-permute-start(bf16[1,128,1024]{2,1,0:T(8,128)(2,1)S(1)} %constant_dynamic-slice_fusion.5), channel_id=1, source_target_pairs={{0,4},{1,5},{2,6},{3,7},{4,0},{5,1},{6,2},{7,3},{8,12},{9,13},{10,... | collective-permute-start | bytes 786440 | tf_op jit(solution)/shard_map/ppermute | solution.py:228
  232.6 15.7 %collective-permute-start.23 = (bf16[2,128,1024]{2,1,0:T(8,128)(2,1)S(1)}, bf16[2,128,1024]{2,1,0:T(8,128)(2,1)S(1)}, u32[]{:S(2)}, u32[]{:S(2)}) collective-permute-start(bf16[2,128,1024]{2,1,0:T(8,128)(2,1)S(1)} %dynamic-slice_bitcast_fusion.3), channel_id=1, source_target_pairs={{0,2},{1,3},{2,0},{3,1},{4,6},{5,7},{6,4},{7,5},{8,10},{9,11},{10,... | collective-permute-start | bytes 1572872 | tf_op jit(solution)/shard_map/ppermute | solution.py:228
  245.3 7.3 %collective-permute-start.26 = (bf16[1,128,1024]{2,1,0:T(8,128)(2,1)S(1)}, bf16[1,128,1024]{2,1,0:T(8,128)(2,1)S(1)}, u32[]{:S(2)}, u32[]{:S(2)}) collective-permute-start(bf16[1,128,1024]{2,1,0:T(8,128)(2,1)S(1)} %constant_dynamic-slice_fusion), channel_id=1, source_target_pairs={{0,2},{1,3},{2,0},{3,1},{4,6},{5,7},{6,4},{7,5},{8,10},{9,11},{10,... | collective-permute-start | bytes 786440 | tf_op jit(solution)/shard_map/ppermute | solution.py:228
  248.4 7.6 %copy-start.1 = (bf16[512,2048]{1,0:T(8,128)(2,1)S(1)}, bf16[512,2048]{1,0:T(8,128)(2,1)}, u32[]{:S(2)}) copy-start(bf16[512,2048]{1,0:T(8,128)(2,1)} %param.28) | copy-start | bytes 6291460
  248.5 6.4 %collective-permute-start.24 = (bf16[1,128,1024]{2,1,0:T(8,128)(2,1)S(1)}, bf16[1,128,1024]{2,1,0:T(8,128)(2,1)S(1)}, u32[]{:S(2)}, u32[]{:S(2)}) collective-permute-start(bf16[1,128,1024]{2,1,0:T(8,128)(2,1)S(1)} %constant_dynamic-slice_fusion.1), channel_id=1, source_target_pairs={{0,4},{1,5},{2,6},{3,7},{4,0},{5,1},{6,2},{7,3},{8,12},{9,13},{10,... | collective-permute-start | bytes 786440 | tf_op jit(solution)/shard_map/ppermute | solution.py:228
  (9 other events, 8.0 us)
Sparse Core Ops, SparseCore 0:
  9.9 46.5 all-gather.2

commit v2 on v1

--- a/solution.py
+++ b/solution.py
@@ -123,7 +123,7 @@
                 rows(2 * value_heads),
                 pl.BlockSpec(start.shape, lambda c, _: (0, 0, 0, 0)),
             ]
-            + [pl.BlockSpec(memory_space=pl.ANY)] * len(unread),
+            + [pl.BlockSpec(memory_space=pltpu.HBM)] * len(unread),
             out_specs=[
                 rows(value_cols),
                 pl.BlockSpec((PAIR, value_heads, LK, LV), lambda c, _: (0, 0, 0, 0)),
@@ -134,7 +134,7 @@
             jax.ShapeDtypeStruct((PAIR, value_heads, LK, LV), f32),
         ],
         input_output_aliases={} if heads is None else {8: 0},
-        compiler_params=pltpu.CompilerParams(vmem_limit_bytes=32 * 2**20),
+        compiler_params=pltpu.CompilerParams(vmem_limit_bytes=60 * 2**20),
         cost_estimate=pl.CostEstimate(flops=10**10, bytes_accessed=3 * 10**6, transcendentals=0),
         name="delta_part",
     )(places, q, k, v, gate, running, columns, start, *unread)
@@ -250,7 +250,8 @@
 
 def project_first(heads, weight, devices, me):
     kept, sent = halves(heads, me, 1, 1)
-    return add(product(kept, weight), swap(product(sent, weight), devices, 1))
+    outgoing = product(sent, weight)
+    return outgoing, add(product(kept, weight), swap(outgoing, devices, 1))
 
 
 def project_next(parts, devices, me):
@@ -373,7 +374,7 @@
     far = swap(near, devices, 1)
 
     block_rows = count * fresh_len // devices
-    total = project_first(heads.reshape(devices, block_rows, -1), delta_out_weight, devices, me)
+    _, total = project_first(heads.reshape(devices, block_rows, -1), delta_out_weight, devices, me)
     scalars = jnp.stack([kv_head, me]).astype(jnp.int32)
     q4 = attn_query.reshape(count, fresh_len // block_rows, block_rows, query_cols)
     gate4 = attn_gate.reshape(q4.shape)
@@ -385,10 +386,10 @@
             chunk, block_rows, devices, q4, gate4, near, far, fresh_all, scalars, lengths, places, deps
         )
         mixed = mixed.reshape(devices, block_rows // CHUNKS, query_cols)
-        total = project_first(mixed, attn_out_weight, devices, me)
+        outgoing, total = project_first(mixed, attn_out_weight, devices, me)
         if parts[0].shape[0] > 1:
             parts = project_next(parts, devices, me)
-        deps = [total, *parts]
+        deps = [outgoing, *parts]
         done.append(total)
     delta_mixed = project_rest(parts, devices, me)
     attn_mixed = [project_rest(column_halves(total), devices, me) for total in done]

time: 267 us -> 235 us (0.88)
  local copies, waits for them, and re-layouts: 40.6 us -> 18.2 us
  waiting for transfers between devices: 71.7 us -> 62.4 us
  Pallas kernels: 56.9 us -> 65.7 us
  other arithmetic: 25.8 us -> 20.7 us
    unnamed x93 -> x55, local copies, waits for them, and re-layouts: 30 us -> 8.48 us
    ppermute x27, waiting for transfers between devices: 71.7 us -> 62.3 us  [swap(): return lax.ppermute(x, axis, [(h, h ^ bit) for h in range(devices)])]
    pallas_call x4, Pallas kernels: 36.7 us -> 45.5 us  [delta_part(): pl.pallas_call(functools.partial(delta_kernel, len(unread)), grid_spec=pl...]
    convert_element_type x9, other arithmetic: 15.1 us -> 7.38 us  [add(): return (a.astype(f32) + b.astype(f32)).astype(bf16)]
  transfers between devices with their start and end apart: 28 -> 28, of which waited for: 11 -> 12; matrix products, arithmetic and copies ran while one was open for 17% -> 16% of each run, Pallas kernels for 14% -> 23%
where the time goes in v2:
time: 235 us; the launch traced here: 232 us
  Pallas kernels  65.7 us (28%)
  waiting for transfers between devices  62.4 us (27%)
  starting transfers between devices  29 us (12%)
  between operations  22.5 us (10%)
  other arithmetic  20.7 us (9%)
  local copies, waits for them, and re-layouts  18.2 us (8%)
  matrix products  13.4 us (6%)
    ppermute x27, waiting for transfers between devices, swap(): return lax.ppermute(x, axis, [(h, h ^ bit) for h in range(devices)])  62.3 us
    pallas_call x4, Pallas kernels, delta_part(): pl.pallas_call(functools.partial(delta_kernel, len(unread)), grid_spec=pl...  45.5 us
    ppermute x27, starting transfers between devices, swap(): return lax.ppermute(x, axis, [(h, h ^ bit) for h in range(devices)])  29 us
    pallas_call x2, Pallas kernels, attend(): pl.pallas_call(functools.partial(attend_kernel, chunk, block_rows, device...  20.2 us
    dot_general x6, matrix products, product(): out = jnp.dot(x.reshape(-1, x.shape[2]), weight, preferred_element_type=f32)  13.1 us
    unnamed x55, local copies, waits for them, and re-layouts  8.48 us
    convert_element_type x9, other arithmetic, add(): return (a.astype(f32) + b.astype(f32)).astype(bf16)  7.38 us
  transfers between devices with their start and end apart: 28, of which 12 were waited for; matrix products, arithmetic and copies ran while one was open for 16% of the time, Pallas kernels for 23%

profile of v2, /device:TPU:0, one launch (start us, length us, event | category | flops | bytes accessed | tf_op | source)
XLA Modules:
  0.0 231.8 jit_solution(4082838862849208399)
XLA Ops:
  7.2 2.0 copy.76
  9.3 0.7 fusion.24
  10.0 0.7 and_select_fusion
  16.4 1.3 convert_element_type.195
  20.2 0.8 constant_dynamic-slice_fusion.17
  21.0 5.1 %collective-permute-start.2 = (bf16[1,4,128,128]{3,2,1,0:T(8,128)(2,1)}, bf16[1,4,128,128]{3,2,1,0:T(8,128)(2,1)}, u32[]{:S(2)}, u32[]{:S(2)}) collective-permute-start(bf16[1,4,128,128]{3,2,1,0:T(8,128)(2,1)} %get-tuple-element.38), channel_id=1, source_target_pairs={{0,24},{8,16},{16,8},{24,0},{1,25},{9,17},{17,9},{25,1},{2,26},{10... | collective-permute-start | bytes 393224 | tf_op jit(solution)/shard_map/ppermute | solution.py:228
  26.6 1.9 constant_dynamic-slice_fusion.12
  28.6 0.9 copy.74
  29.4 1.7 collective-permute-start.3
  31.5 1.3 copy.55
  33.0 0.6 fusion.31
  33.6 3.8 %collective-permute-done.1 = bf16[1,4,128,128]{3,2,1,0:T(8,128)(2,1)} collective-permute-done((bf16[1,4,128,128]{3,2,1,0:T(8,128)(2,1)}, bf16[1,4,128,128]{3,2,1,0:T(8,128)(2,1)}, u32[]{:S(2)}, u32[]{:S(2)}) %collective-permute-start.1) | collective-permute-done | bytes 131104 | tf_op jit(solution)/shard_map/ppermute | solution.py:228
  37.5 1.9 pad_maximum_fusion.3.start_ref
  39.3 12.0 %collective-permute-done.3 = bf16[4,2,128,256]{3,2,1,0:T(8,128)(2,1)} collective-permute-done((bf16[4,2,128,256]{3,2,1,0:T(8,128)(2,1)}, bf16[4,2,128,256]{3,2,1,0:T(8,128)(2,1)}, u32[]{:S(2)}, u32[]{:S(2)}) %collective-permute-start.3) | collective-permute-done | bytes 524320 | tf_op jit(solution)/shard_map/ppermute | solution.py:228
  51.3 2.0 fusion.15
  53.3 1.0 collective-permute-start.4
  54.3 3.2 %collective-permute-start.6 = (bf16[1,2,2,128,256]{4,3,2,1,0:T(8,128)(2,1)}, bf16[1,2,2,128,256]{4,3,2,1,0:T(8,128)(2,1)S(1)}, u32[]{:S(2)}, u32[]{:S(2)}) collective-permute-start(bf16[1,2,2,128,256]{4,3,2,1,0:T(8,128)(2,1)} %get-tuple-element.33), channel_id=1, source_target_pairs={{0,16},{8,24},{16,0},{24,8},{1,17},{9,25},{17,1},{25,9},{2,18},{10... | collective-permute-start | bytes 786440 | tf_op jit(solution)/shard_map/ppermute | solution.py:228
  57.5 11.7 %delta_part.4 = (bf16[4,512,512]{2,1,0:T(8,128)(2,1)}, f32[2,4,128,128]{3,2,1,0:T(8,128)}) custom-call(s32[2]{0:T(128)} %get-tuple-element.41.source, bf16[4,512,256]{2,1,0:T(8,128)(2,1)} %q_ref.7, bf16[4,512,256]{2,1,0:T(8,128)(2,1)} %k_ref.7, bf16[4,512,512]{2,1,0:T(8,128)(2,1)} %v_ref.7, bf16[4,512,512]{2,1,0:T(8,128)(2,1)} %gate_ref.7, ...), custom_call_target="tpu_custom_call" | custom-call | flops 10000000000 | bytes 3000000 | tf_op jit(solution)/shard_map/delta_part/pallas_call | solution.py:112
  69.2 1.6 collective-permute-start.7
  70.9 0.7 collective-permute-start.5
  71.5 1.4 collective-permute-start.8
  73.5 11.2 %delta_part.5 = (bf16[4,512,512]{2,1,0:T(8,128)(2,1)}, f32[2,4,128,128]{3,2,1,0:T(8,128)}) custom-call(s32[2]{0:T(128)} %iota.35.source, bf16[4,512,256]{2,1,0:T(8,128)(2,1)} %q_ref.7, bf16[4,512,256]{2,1,0:T(8,128)(2,1)} %k_ref.7, bf16[4,512,512]{2,1,0:T(8,128)(2,1)} %v_ref.7, bf16[4,512,512]{2,1,0:T(8,128)(2,1)} %gate_ref.7, ...), custom_call_target="tpu_custom_call", output_to_operand_aliasing={{0}: (8, {})} | custom-call | flops 10000000000 | bytes 3000000 | tf_op jit(solution)/shard_map/delta_part/pallas_call | solution.py:112
  84.8 0.7 copy-done.11
  85.5 11.2 %delta_part.6 = (bf16[4,512,512]{2,1,0:T(8,128)(2,1)}, f32[2,4,128,128]{3,2,1,0:T(8,128)}) custom-call(s32[2]{0:T(128)} %get-tuple-element.42.source, bf16[4,512,256]{2,1,0:T(8,128)(2,1)} %q_ref.7, bf16[4,512,256]{2,1,0:T(8,128)(2,1)} %k_ref.7, bf16[4,512,512]{2,1,0:T(8,128)(2,1)} %v_ref.7, ...), custom_call_target="tpu_custom_call", output_to_operand_aliasing={{0}: (8, {})} | custom-call | flops 10000000000 | bytes 3000000 | tf_op jit(solution)/shard_map/delta_part/pallas_call | solution.py:112
  97.5 11.4 %delta_part.7 = (bf16[4,512,512]{2,1,0:T(8,128)(2,1)}, f32[2,4,128,128]{3,2,1,0:T(8,128)}) custom-call(s32[2]{0:T(128)} %iota.30.source, bf16[4,512,256]{2,1,0:T(8,128)(2,1)} %q_ref.7, bf16[4,512,256]{2,1,0:T(8,128)(2,1)} %k_ref.7, bf16[4,512,512]{2,1,0:T(8,128)(2,1)} %v_ref.7, bf16[4,512,512]{2,1,0:T(8,128)(2,1)} %gate_ref.7, ...), custom_call_target="tpu_custom_call", output_to_operand_aliasing={{0}: (8, {})} | custom-call | flops 10000000000 | bytes 3000000 | tf_op jit(solution)/shard_map/delta_part/pallas_call | solution.py:112
  108.9 1.7 constant_dynamic-slice_fusion.10
  110.7 4.3 %convolution_convert_fusion = bf16[1024,2048]{1,0:T(8,128)(2,1)} fusion(bf16[1024,512]{1,0:T(8,128)(2,1)S(1)} %bitcast.142, bf16[512,2048]{1,0:T(8,128)(2,1)S(1)} %copy-done), kind=kOutput, calls=%fused_computation.6 | convolution fusion | flops 2149580800 | bytes 7340032 | tf_op jit(solution)/shard_map/dot_general | solution.py:247
  115.6 8.1 %collective-permute-done.15 = bf16[1,2,2,128,256]{4,3,2,1,0:T(8,128)(2,1)S(1)} collective-permute-done((bf16[1,2,2,128,256]{4,3,2,1,0:T(8,128)(2,1)S(1)}, bf16[1,2,2,128,256]{4,3,2,1,0:T(8,128)(2,1)S(1)}, u32[]{:S(2)}, u32[]{:S(2)}) %collective-permute-start.15) | collective-permute-done | bytes 262176 | tf_op jit(solution)/shard_map/ppermute | solution.py:228
  123.8 1.4 maximum_maximum_fusion.near_ref
  125.3 2.3 pad_maximum_fusion.2
  127.6 2.4 %convolution_convert_fusion.1 = bf16[1024,2048]{1,0:T(8,128)(2,1)S(1)} fusion(bf16[1024,512]{1,0:T(8,128)(2,1)S(1)} %bitcast.141, bf16[512,2048]{1,0:T(8,128)(2,1)S(1)} %copy-done), kind=kOutput, calls=%fused_computation.7 | convolution fusion | flops 2149580800 | bytes 7340032 | tf_op jit(solution)/shard_map/dot_general | solution.py:247
  130.0 4.1 %fusion.refs_0_ = bf16[4,256,2048]{2,1,0:T(8,128)(2,1)S(1)} fusion(bf16[4,256,2048]{2,1,0:T(8,128)(2,1)S(1)} %bitcast.127, bf16[4,256,2048]{2,1,0:T(8,128)(2,1)} %collective-permute-done.10), kind=kLoop, calls=%fused_computation.1 | loop fusion | flops 8388608 | bytes 12582912 | tf_op jit(solution)/shard_map/convert_element_type | solution.py:243
  134.1 0.6 fusion.28
  134.7 1.5 copy-done.4
  136.2 2.5 %collective-permute-start.13 = (bf16[2,256,1024]{2,1,0:T(8,128)(2,1)S(1)}, bf16[2,256,1024]{2,1,0:T(8,128)(2,1)S(1)}, u32[]{:S(2)}, u32[]{:S(2)}) collective-permute-start(bf16[2,256,1024]{2,1,0:T(8,128)(2,1)S(1)} %dynamic-slice_bitcast_fusion), channel_id=1, source_target_pairs={{0,4},{1,5},{2,6},{3,7},{4,0},{5,1},{6,2},{7,3},{8,12},{9,13},{10,... | collective-permute-start | bytes 3145736 | tf_op jit(solution)/shard_map/ppermute | solution.py:228
  138.8 0.7 collective-permute-start.11
  139.5 10.0 %attend.2 = bf16[4,2,128,512]{3,2,1,0:T(8,128)(2,1)S(1)} custom-call(s32[6]{0:T(128)S(1)} %pad_add_fusion.scalars, s32[4]{0:T(128)S(1)} %dynamic_slice.167.lengths, bf16[4,2,256,512]{3,2,1,0:T(8,128)(2,1)S(1)} %bitcast.119, bf16[4,2,256,512]{3,2,1,0:T(8,128)(2,1)S(1)} %bitcast.122, bf16[4,4,2,128,256]{4,3,2,1,0:T(8,128)(2,1)} %maximum_maximum_fusion.near_ref, ...), custom_call_target="tpu_custom_call" | custom-call | flops 10000000000 | bytes 8000000 | tf_op jit(solution)/shard_map/attend/pallas_call | solution.py:203
  149.7 1.5 copy-done.23
  151.2 2.6 %convolution_convert_fusion.4 = bf16[512,2048]{1,0:T(8,128)(2,1)} fusion(bf16[512,512]{1,0:T(8,128)(2,1)S(1)} %bitcast.151, bf16[512,2048]{1,0:T(8,128)(2,1)S(1)} %copy-done.23), kind=kOutput, calls=%fused_computation.10 | convolution fusion | flops 1074790400 | bytes 4718592 | tf_op jit(solution)/shard_map/dot_general | solution.py:247
  153.9 1.3 convolution_convert_fusion.5
  155.2 7.4 %collective-permute-done.13 = bf16[2,256,1024]{2,1,0:T(8,128)(2,1)S(1)} collective-permute-done((bf16[2,256,1024]{2,1,0:T(8,128)(2,1)S(1)}, bf16[2,256,1024]{2,1,0:T(8,128)(2,1)S(1)}, u32[]{:S(2)}, u32[]{:S(2)}) %collective-permute-start.13) | collective-permute-done | bytes 1048608 | tf_op jit(solution)/shard_map/ppermute | solution.py:228
  163.0 0.7 collective-permute-start.14
  164.6 1.4 collective-permute-start.12
  166.0 10.2 %attend.3 = bf16[4,2,128,512]{3,2,1,0:T(8,128)(2,1)S(1)} custom-call(s32[6]{0:T(128)S(1)} %pad_add_fusion.scalars, s32[4]{0:T(128)S(1)} %dynamic_slice.167.lengths, bf16[4,2,256,512]{3,2,1,0:T(8,128)(2,1)S(1)} %bitcast.120, bf16[4,2,256,512]{3,2,1,0:T(8,128)(2,1)} %bitcast.121, bf16[4,4,2,128,256]{4,3,2,1,0:T(8,128)(2,1)} %maximum_maximum_fusion.near_ref, ...), custom_call_target="tpu_custom_call" | custom-call | flops 10000000000 | bytes 8000000 | tf_op jit(solution)/shard_map/attend/pallas_call | solution.py:203
  176.3 1.5 copy-done.24
  177.8 1.3 convolution_convert_fusion.2
  179.1 1.3 convolution_convert_fusion.3
  180.6 0.9 fusion.2
  181.8 0.8 collective-permute-start.20
  182.7 1.1 pad_maximum_fusion
  183.8 1.0 collective-permute-start.18
  184.8 11.3 %collective-permute-done.20 = bf16[2,128,1024]{2,1,0:T(8,128)(2,1)S(1)} collective-permute-done((bf16[2,128,1024]{2,1,0:T(8,128)(2,1)S(1)}, bf16[2,128,1024]{2,1,0:T(8,128)(2,1)S(1)}, u32[]{:S(2)}, u32[]{:S(2)}) %collective-permute-start.20) | collective-permute-done | bytes 524320 | tf_op jit(solution)/shard_map/ppermute | solution.py:228
  196.4 1.4 collective-permute-start.21
  197.8 0.8 fusion.1
  199.5 1.8 collective-permute-start.19
  201.3 0.7 collective-permute-start.23
  202.1 3.6 %collective-permute-done.21 = bf16[1,128,1024]{2,1,0:T(8,128)(2,1)S(1)} collective-permute-done((bf16[1,128,1024]{2,1,0:T(8,128)(2,1)S(1)}, bf16[1,128,1024]{2,1,0:T(8,128)(2,1)S(1)}, u32[]{:S(2)}, u32[]{:S(2)}) %collective-permute-start.21) | collective-permute-done | bytes 262176 | tf_op jit(solution)/shard_map/ppermute | solution.py:228
  205.7 8.1 %collective-permute-done.25 = bf16[2,128,1024]{2,1,0:T(8,128)(2,1)S(1)} collective-permute-done((bf16[2,128,1024]{2,1,0:T(8,128)(2,1)S(1)}, bf16[2,128,1024]{2,1,0:T(8,128)(2,1)S(1)}, u32[]{:S(2)}, u32[]{:S(2)}) %collective-permute-start.25) | collective-permute-done | bytes 524320 | tf_op jit(solution)/shard_map/ppermute | solution.py:228
  214.1 0.7 collective-permute-start.26
  214.8 2.1 collective-permute-done.23
  217.1 0.8 collective-permute-start.24
  218.3 2.9 %collective-permute-done.26 = bf16[1,128,1024]{2,1,0:T(8,128)(2,1)S(1)} collective-permute-done((bf16[1,128,1024]{2,1,0:T(8,128)(2,1)S(1)}, bf16[1,128,1024]{2,1,0:T(8,128)(2,1)S(1)}, u32[]{:S(2)}, u32[]{:S(2)}) %collective-permute-start.26) | collective-permute-done | bytes 262176 | tf_op jit(solution)/shard_map/ppermute | solution.py:228
  221.3 2.3 collective-permute-done.24
  223.7 1.1 maximum_maximum_fusion.1
  (118 shorter events, 8.7 us)
Async XLA Ops:
  7.2 103.4 %copy-start = (bf16[512,2048]{1,0:T(8,128)(2,1)S(1)}, bf16[512,2048]{1,0:T(8,128)(2,1)}, u32[]{:S(2)}) copy-start(bf16[512,2048]{1,0:T(8,128)(2,1)} %param.28) | copy-start | bytes 6291460
  7.2 89.6 %all-gather.3.cloned.1.call-start = ((), (), s32[]{:S(2)}) async-start(), calls=%async_computation | async-start | bytes 4718592 | tf_op jit(solution)/shard_map/all_gather | solution.py:323
  20.2 10.9 %copy-start.20 = (f32[4,4,512]{2,1,0:T(4,128)S(1)}, f32[4,4,512]{2,1,0:T(4,128)}, u32[]{:S(2)}) copy-start(f32[4,4,512]{2,1,0:T(4,128)} %param.20) | copy-start | bytes 98308
  20.2 11.2 %copy-start.21 = (f32[4,4,512]{2,1,0:T(4,128)S(1)}, f32[4,4,512]{2,1,0:T(4,128)}, u32[]{:S(2)}) copy-start(f32[4,4,512]{2,1,0:T(4,128)} %param.19) | copy-start | bytes 98308
  21.0 12.6 %collective-permute-start.2 = (bf16[1,4,128,128]{3,2,1,0:T(8,128)(2,1)}, bf16[1,4,128,128]{3,2,1,0:T(8,128)(2,1)}, u32[]{:S(2)}, u32[]{:S(2)}) collective-permute-start(bf16[1,4,128,128]{3,2,1,0:T(8,128)(2,1)} %get-tuple-element.38), channel_id=1, source_target_pairs={{0,24},{8,16},{16,8},{24,0},{1,25},{9,17},{17,9},{25,1},{2,26},{10... | collective-permute-start | bytes 393224 | tf_op jit(solution)/shard_map/ppermute | solution.py:228
  26.1 11.4 %collective-permute-start.1 = (bf16[1,4,128,128]{3,2,1,0:T(8,128)(2,1)}, bf16[1,4,128,128]{3,2,1,0:T(8,128)(2,1)}, u32[]{:S(2)}, u32[]{:S(2)}) collective-permute-start(bf16[1,4,128,128]{3,2,1,0:T(8,128)(2,1)} %get-tuple-element.39), channel_id=1, source_target_pairs={{0,16},{8,24},{16,0},{24,8},{1,17},{9,25},{17,1},{25,9},{2,18},{10... | collective-permute-start | bytes 393224 | tf_op jit(solution)/shard_map/ppermute | solution.py:228
  26.1 11.4 %collective-permute-start = (bf16[1,4,128,128]{3,2,1,0:T(8,128)(2,1)S(1)}, bf16[1,4,128,128]{3,2,1,0:T(8,128)(2,1)}, u32[]{:S(2)}, u32[]{:S(2)}) collective-permute-start(bf16[1,4,128,128]{3,2,1,0:T(8,128)(2,1)S(1)} %get-tuple-element.40), channel_id=1, source_target_pairs={{0,8},{8,0},{16,24},{24,16},{1,9},{9,1},{17,25},{25,17},{2,10},{10... | collective-permute-start | bytes 393224 | tf_op jit(solution)/shard_map/ppermute | solution.py:228
  28.5 4.4 %copy-start.22 = (s32[16]{0:T(128)S(1)}, s32[16]{0:T(128)}, u32[]{:S(2)}) copy-start(s32[16]{0:T(128)} %param.27) | copy-start | bytes 196
  29.4 21.9 %collective-permute-start.3 = (bf16[4,2,128,256]{3,2,1,0:T(8,128)(2,1)}, bf16[4,2,128,256]{3,2,1,0:T(8,128)(2,1)}, u32[]{:S(2)}, u32[]{:S(2)}) collective-permute-start(bf16[4,2,128,256]{3,2,1,0:T(8,128)(2,1)} %bitcast.116), channel_id=1, source_target_pairs={{0,4},{1,5},{2,6},{3,7},{4,0},{5,1},{6,2},{7,3},{8,12},{9,13},{10,... | collective-permute-start | bytes 1572872 | tf_op jit(solution)/shard_map/ppermute | solution.py:228
  31.5 21.9 %copy-start.19 = (f32[4,4,512]{2,1,0:T(4,128)}, f32[4,4,512]{2,1,0:T(4,128)S(1)}, u32[]{:S(2)}) copy-start(f32[4,4,512]{2,1,0:T(4,128)S(1)} %reshape.199.row_ref) | copy-start | bytes 98308
  53.3 17.5 %collective-permute-start.4 = (bf16[1,2,2,128,256]{4,3,2,1,0:T(8,128)(2,1)}, bf16[1,2,2,128,256]{4,3,2,1,0:T(8,128)(2,1)S(1)}, u32[]{:S(2)}, u32[]{:S(2)}) collective-permute-start(bf16[1,2,2,128,256]{4,3,2,1,0:T(8,128)(2,1)} %get-tuple-element.32), channel_id=1, source_target_pairs={{0,8},{8,0},{16,24},{24,16},{1,9},{9,1},{17,25},{25,17},{2,10},{10... | collective-permute-start | bytes 786440 | tf_op jit(solution)/shard_map/ppermute | solution.py:228
  54.3 17.2 %collective-permute-start.6 = (bf16[1,2,2,128,256]{4,3,2,1,0:T(8,128)(2,1)}, bf16[1,2,2,128,256]{4,3,2,1,0:T(8,128)(2,1)S(1)}, u32[]{:S(2)}, u32[]{:S(2)}) collective-permute-start(bf16[1,2,2,128,256]{4,3,2,1,0:T(8,128)(2,1)} %get-tuple-element.33), channel_id=1, source_target_pairs={{0,16},{8,24},{16,0},{24,8},{1,17},{9,25},{17,1},{25,9},{2,18},{10... | collective-permute-start | bytes 786440 | tf_op jit(solution)/shard_map/ppermute | solution.py:228
  69.2 15.5 %collective-permute-start.7 = (bf16[1,2,2,128,256]{4,3,2,1,0:T(8,128)(2,1)S(1)}, bf16[1,2,2,128,256]{4,3,2,1,0:T(8,128)(2,1)S(1)}, u32[]{:S(2)}, u32[]{:S(2)}) collective-permute-start(bf16[1,2,2,128,256]{4,3,2,1,0:T(8,128)(2,1)S(1)} %get-tuple-element.34), channel_id=1, source_target_pairs={{0,2},{1,3},{2,0},{3,1},{4,6},{5,7},{6,4},{7,5},{8,10},{9,11},{10,... | collective-permute-start | bytes 786440 | tf_op jit(solution)/shard_map/ppermute | solution.py:228
  70.9 25.8 %collective-permute-start.9 = (bf16[1,2,2,128,256]{4,3,2,1,0:T(8,128)(2,1)}, bf16[1,2,2,128,256]{4,3,2,1,0:T(8,128)(2,1)S(1)}, u32[]{:S(2)}, u32[]{:S(2)}) collective-permute-start(bf16[1,2,2,128,256]{4,3,2,1,0:T(8,128)(2,1)} %get-tuple-element.31), channel_id=1, source_target_pairs={{0,24},{8,16},{16,8},{24,0},{1,25},{9,17},{17,9},{25,1},{2,26},{10... | collective-permute-start | bytes 786440 | tf_op jit(solution)/shard_map/ppermute | solution.py:228
  70.9 2.6 %copy-start.7 = (bf16[1,2,2,128,256]{4,3,2,1,0:T(8,128)(2,1)}, bf16[1,2,2,128,256]{4,3,2,1,0:T(8,128)(2,1)S(1)}, u32[]{:S(2)}) copy-start(bf16[1,2,2,128,256]{4,3,2,1,0:T(8,128)(2,1)S(1)} %collective-permute-done.4.refs_1_) | copy-start | bytes 786436
  70.9 13.8 %collective-permute-start.5 = (bf16[1,2,2,128,256]{4,3,2,1,0:T(8,128)(2,1)S(1)}, bf16[1,2,2,128,256]{4,3,2,1,0:T(8,128)(2,1)S(1)}, u32[]{:S(2)}, u32[]{:S(2)}) collective-permute-start(bf16[1,2,2,128,256]{4,3,2,1,0:T(8,128)(2,1)S(1)} %collective-permute-done.4.refs_1_), channel_id=1, source_target_pairs={{0,2},{1,3},{2,0},{3,1},{4,6},{5,7},{6,4},{7,5},{8,10},{9,11},{10,... | collective-permute-start | bytes 786440 | tf_op jit(solution)/shard_map/ppermute | solution.py:228
  71.5 13.2 %copy-start.9 = (bf16[1,2,2,128,256]{4,3,2,1,0:T(8,128)(2,1)}, bf16[1,2,2,128,256]{4,3,2,1,0:T(8,128)(2,1)S(1)}, u32[]{:S(2)}) copy-start(bf16[1,2,2,128,256]{4,3,2,1,0:T(8,128)(2,1)S(1)} %collective-permute-done.6.refs_2_) | copy-start | bytes 786436
  71.5 25.2 %collective-permute-start.8 = (bf16[1,2,2,128,256]{4,3,2,1,0:T(8,128)(2,1)S(1)}, bf16[1,2,2,128,256]{4,3,2,1,0:T(8,128)(2,1)S(1)}, u32[]{:S(2)}, u32[]{:S(2)}) collective-permute-start(bf16[1,2,2,128,256]{4,3,2,1,0:T(8,128)(2,1)S(1)} %collective-permute-done.6.refs_2_), channel_id=1, source_target_pairs={{0,2},{1,3},{2,0},{3,1},{4,6},{5,7},{6,4},{7,5},{8,10},{9,11},{10,... | collective-permute-start | bytes 786440 | tf_op jit(solution)/shard_map/ppermute | solution.py:228
  84.7 0.7 copy-start.11
  84.7 0.8 copy-start.15
  96.7 0.7 copy-start.13
  96.7 0.8 copy-start.17
  110.6 4.4 %copy-start.14 = (bf16[1,2,2,128,256]{4,3,2,1,0:T(8,128)(2,1)S(1)}, bf16[1,2,2,128,256]{4,3,2,1,0:T(8,128)(2,1)}, u32[]{:S(2)}) copy-start(bf16[1,2,2,128,256]{4,3,2,1,0:T(8,128)(2,1)} %copy-done.13) | copy-start | bytes 786436
  110.6 13.1 %copy-start.8 = (bf16[1,2,2,128,256]{4,3,2,1,0:T(8,128)(2,1)S(1)}, bf16[1,2,2,128,256]{4,3,2,1,0:T(8,128)(2,1)}, u32[]{:S(2)}) copy-start(bf16[1,2,2,128,256]{4,3,2,1,0:T(8,128)(2,1)} %copy-done.7) | copy-start | bytes 786436
  110.6 13.1 %copy-start.10 = (bf16[1,2,2,128,256]{4,3,2,1,0:T(8,128)(2,1)S(1)}, bf16[1,2,2,128,256]{4,3,2,1,0:T(8,128)(2,1)}, u32[]{:S(2)}) copy-start(bf16[1,2,2,128,256]{4,3,2,1,0:T(8,128)(2,1)} %copy-done.9) | copy-start | bytes 786436
  110.6 13.1 %copy-start.12 = (bf16[1,2,2,128,256]{4,3,2,1,0:T(8,128)(2,1)S(1)}, bf16[1,2,2,128,256]{4,3,2,1,0:T(8,128)(2,1)}, u32[]{:S(2)}) copy-start(bf16[1,2,2,128,256]{4,3,2,1,0:T(8,128)(2,1)} %copy-done.11) | copy-start | bytes 786436
  110.6 13.1 %copy-start.16 = (bf16[1,2,2,128,256]{4,3,2,1,0:T(8,128)(2,1)S(1)}, bf16[1,2,2,128,256]{4,3,2,1,0:T(8,128)(2,1)}, u32[]{:S(2)}) copy-start(bf16[1,2,2,128,256]{4,3,2,1,0:T(8,128)(2,1)} %copy-done.15) | copy-start | bytes 786436
  110.6 13.1 %copy-start.18 = (bf16[1,2,2,128,256]{4,3,2,1,0:T(8,128)(2,1)S(1)}, bf16[1,2,2,128,256]{4,3,2,1,0:T(8,128)(2,1)}, u32[]{:S(2)}) copy-start(bf16[1,2,2,128,256]{4,3,2,1,0:T(8,128)(2,1)} %copy-done.17) | copy-start | bytes 786436
  115.0 15.0 %collective-permute-start.10 = (bf16[4,256,2048]{2,1,0:T(8,128)(2,1)}, bf16[4,256,2048]{2,1,0:T(8,128)(2,1)}, u32[]{:S(2)}, u32[]{:S(2)}) collective-permute-start(bf16[4,256,2048]{2,1,0:T(8,128)(2,1)} %bitcast.16), channel_id=1, source_target_pairs={{0,1},{1,0},{2,3},{3,2},{4,5},{5,4},{6,7},{7,6},{8,9},{9,8},{10,11... | collective-permute-start | bytes 12582920 | tf_op jit(solution)/shard_map/ppermute | solution.py:228
  115.0 8.7 %collective-permute-start.15 = (bf16[1,2,2,128,256]{4,3,2,1,0:T(8,128)(2,1)S(1)}, bf16[1,2,2,128,256]{4,3,2,1,0:T(8,128)(2,1)S(1)}, u32[]{:S(2)}, u32[]{:S(2)}) collective-permute-start(bf16[1,2,2,128,256]{4,3,2,1,0:T(8,128)(2,1)S(1)} %copy-done.14), channel_id=1, source_target_pairs={{0,2},{1,3},{2,0},{3,1},{4,6},{5,7},{6,4},{7,5},{8,10},{9,11},{10,... | collective-permute-start | bytes 786440 | tf_op jit(solution)/shard_map/ppermute | solution.py:228
  123.8 1.5 copy-start.25
  125.1 14.4 %collective-permute-start.16 = (bf16[4,4,2,128,256]{4,3,2,1,0:T(8,128)(2,1)}, bf16[4,4,2,128,256]{4,3,2,1,0:T(8,128)(2,1)}, u32[]{:S(2)}, u32[]{:S(2)}) collective-permute-start(bf16[4,4,2,128,256]{4,3,2,1,0:T(8,128)(2,1)} %maximum_maximum_fusion.near_ref), channel_id=1, source_target_pairs={{0,1},{1,0},{2,3},{3,2},{4,5},{5,4},{6,7},{7,6},{8,9},{9,8},{10,11... | collective-permute-start | bytes 6291464 | tf_op jit(solution)/shard_map/ppermute | solution.py:228
  134.1 2.1 copy-start.4
  136.2 2.6 %copy-start.5 = (bf16[4,256,1024]{2,1,0:T(8,128)(2,1)}, bf16[4,256,1024]{2,1,0:T(8,128)(2,1)S(1)}, u32[]{:S(2)}) copy-start(bf16[4,256,1024]{2,1,0:T(8,128)(2,1)S(1)} %get-tuple-element.20) | copy-start | bytes 6291460
  136.2 3.4 %copy-start.2 = (bf16[4,512,512]{2,1,0:T(8,128)(2,1)S(1)}, bf16[4,512,512]{2,1,0:T(8,128)(2,1)}, u32[]{:S(2)}) copy-start(bf16[4,512,512]{2,1,0:T(8,128)(2,1)} %param.24) | copy-start | bytes 6291460
  136.2 3.4 %copy-start.3 = (bf16[4,512,512]{2,1,0:T(8,128)(2,1)S(1)}, bf16[4,512,512]{2,1,0:T(8,128)(2,1)}, u32[]{:S(2)}) copy-start(bf16[4,512,512]{2,1,0:T(8,128)(2,1)} %param.25) | copy-start | bytes 6291460
  136.2 26.3 %collective-permute-start.13 = (bf16[2,256,1024]{2,1,0:T(8,128)(2,1)S(1)}, bf16[2,256,1024]{2,1,0:T(8,128)(2,1)S(1)}, u32[]{:S(2)}, u32[]{:S(2)}) collective-permute-start(bf16[2,256,1024]{2,1,0:T(8,128)(2,1)S(1)} %dynamic-slice_bitcast_fusion), channel_id=1, source_target_pairs={{0,4},{1,5},{2,6},{3,7},{4,0},{5,1},{6,2},{7,3},{8,12},{9,13},{10,... | collective-permute-start | bytes 3145736 | tf_op jit(solution)/shard_map/ppermute | solution.py:228
  138.8 25.4 %collective-permute-start.11 = (bf16[2,256,1024]{2,1,0:T(8,128)(2,1)S(1)}, bf16[2,256,1024]{2,1,0:T(8,128)(2,1)S(1)}, u32[]{:S(2)}, u32[]{:S(2)}) collective-permute-start(bf16[2,256,1024]{2,1,0:T(8,128)(2,1)S(1)} %dynamic-slice_bitcast_fusion.1), channel_id=1, source_target_pairs={{0,2},{1,3},{2,0},{3,1},{4,6},{5,7},{6,4},{7,5},{8,10},{9,11},{10,... | collective-permute-start | bytes 3145736 | tf_op jit(solution)/shard_map/ppermute | solution.py:228
  149.6 1.6 copy-start.23
  153.8 26.8 %collective-permute-start.17 = (bf16[4,128,2048]{2,1,0:T(8,128)(2,1)}, bf16[4,128,2048]{2,1,0:T(8,128)(2,1)S(1)}, u32[]{:S(2)}, u32[]{:S(2)}) collective-permute-start(bf16[4,128,2048]{2,1,0:T(8,128)(2,1)} %bitcast.43.refs_0_), channel_id=1, source_target_pairs={{0,1},{1,0},{2,3},{3,2},{4,5},{5,4},{6,7},{7,6},{8,9},{9,8},{10,11... | collective-permute-start | bytes 6291464 | tf_op jit(solution)/shard_map/ppermute | solution.py:228
  153.9 8.6 %copy-start.6 = (bf16[4,256,1024]{2,1,0:T(8,128)(2,1)S(1)}, bf16[4,256,1024]{2,1,0:T(8,128)(2,1)}, u32[]{:S(2)}) copy-start(bf16[4,256,1024]{2,1,0:T(8,128)(2,1)} %copy-done.5) | copy-start | bytes 6291460
  163.0 17.4 %collective-permute-start.14 = (bf16[1,256,1024]{2,1,0:T(8,128)(2,1)S(1)}, bf16[1,256,1024]{2,1,0:T(8,128)(2,1)S(1)}, u32[]{:S(2)}, u32[]{:S(2)}) collective-permute-start(bf16[1,256,1024]{2,1,0:T(8,128)(2,1)S(1)} %constant_dynamic-slice_fusion.8), channel_id=1, source_target_pairs={{0,2},{1,3},{2,0},{3,1},{4,6},{5,7},{6,4},{7,5},{8,10},{9,11},{10,... | collective-permute-start | bytes 1572872 | tf_op jit(solution)/shard_map/ppermute | solution.py:228
  164.6 17.9 %collective-permute-start.12 = (bf16[1,256,1024]{2,1,0:T(8,128)(2,1)S(1)}, bf16[1,256,1024]{2,1,0:T(8,128)(2,1)S(1)}, u32[]{:S(2)}, u32[]{:S(2)}) collective-permute-start(bf16[1,256,1024]{2,1,0:T(8,128)(2,1)S(1)} %constant_dynamic-slice_fusion.9), channel_id=1, source_target_pairs={{0,4},{1,5},{2,6},{3,7},{4,0},{5,1},{6,2},{7,3},{8,12},{9,13},{10,... | collective-permute-start | bytes 1572872 | tf_op jit(solution)/shard_map/ppermute | solution.py:228
  176.2 1.6 copy-start.24
  179.0 18.8 %collective-permute-start.22 = (bf16[4,128,2048]{2,1,0:T(8,128)(2,1)S(1)}, bf16[4,128,2048]{2,1,0:T(8,128)(2,1)S(1)}, u32[]{:S(2)}, u32[]{:S(2)}) collective-permute-start(bf16[4,128,2048]{2,1,0:T(8,128)(2,1)S(1)} %bitcast.162), channel_id=1, source_target_pairs={{0,1},{1,0},{2,3},{3,2},{4,5},{5,4},{6,7},{7,6},{8,9},{9,8},{10,11... | collective-permute-start | bytes 6291464 | tf_op jit(solution)/shard_map/ppermute | solution.py:228
  181.8 14.4 %collective-permute-start.20 = (bf16[2,128,1024]{2,1,0:T(8,128)(2,1)S(1)}, bf16[2,128,1024]{2,1,0:T(8,128)(2,1)S(1)}, u32[]{:S(2)}, u32[]{:S(2)}) collective-permute-start(bf16[2,128,1024]{2,1,0:T(8,128)(2,1)S(1)} %dynamic-slice_bitcast_fusion.4), channel_id=1, source_target_pairs={{0,4},{1,5},{2,6},{3,7},{4,0},{5,1},{6,2},{7,3},{8,12},{9,13},{10,... | collective-permute-start | bytes 1572872 | tf_op jit(solution)/shard_map/ppermute | solution.py:228
  183.8 15.4 %collective-permute-start.18 = (bf16[2,128,1024]{2,1,0:T(8,128)(2,1)S(1)}, bf16[2,128,1024]{2,1,0:T(8,128)(2,1)S(1)}, u32[]{:S(2)}, u32[]{:S(2)}) collective-permute-start(bf16[2,128,1024]{2,1,0:T(8,128)(2,1)S(1)} %dynamic-slice_bitcast_fusion.5), channel_id=1, source_target_pairs={{0,2},{1,3},{2,0},{3,1},{4,6},{5,7},{6,4},{7,5},{8,10},{9,11},{10,... | collective-permute-start | bytes 1572872 | tf_op jit(solution)/shard_map/ppermute | solution.py:228
  196.4 9.3 %collective-permute-start.21 = (bf16[1,128,1024]{2,1,0:T(8,128)(2,1)S(1)}, bf16[1,128,1024]{2,1,0:T(8,128)(2,1)S(1)}, u32[]{:S(2)}, u32[]{:S(2)}) collective-permute-start(bf16[1,128,1024]{2,1,0:T(8,128)(2,1)S(1)} %constant_dynamic-slice_fusion.4), channel_id=1, source_target_pairs={{0,2},{1,3},{2,0},{3,1},{4,6},{5,7},{6,4},{7,5},{8,10},{9,11},{10,... | collective-permute-start | bytes 786440 | tf_op jit(solution)/shard_map/ppermute | solution.py:228
  198.9 14.9 %collective-permute-start.25 = (bf16[2,128,1024]{2,1,0:T(8,128)(2,1)S(1)}, bf16[2,128,1024]{2,1,0:T(8,128)(2,1)S(1)}, u32[]{:S(2)}, u32[]{:S(2)}) collective-permute-start(bf16[2,128,1024]{2,1,0:T(8,128)(2,1)S(1)} %dynamic-slice_bitcast_fusion.2), channel_id=1, source_target_pairs={{0,4},{1,5},{2,6},{3,7},{4,0},{5,1},{6,2},{7,3},{8,12},{9,13},{10,... | collective-permute-start | bytes 1572872 | tf_op jit(solution)/shard_map/ppermute | solution.py:228
  199.5 18.8 %collective-permute-start.19 = (bf16[1,128,1024]{2,1,0:T(8,128)(2,1)S(1)}, bf16[1,128,1024]{2,1,0:T(8,128)(2,1)S(1)}, u32[]{:S(2)}, u32[]{:S(2)}) collective-permute-start(bf16[1,128,1024]{2,1,0:T(8,128)(2,1)S(1)} %constant_dynamic-slice_fusion.5), channel_id=1, source_target_pairs={{0,4},{1,5},{2,6},{3,7},{4,0},{5,1},{6,2},{7,3},{8,12},{9,13},{10,... | collective-permute-start | bytes 786440 | tf_op jit(solution)/shard_map/ppermute | solution.py:228
  201.3 15.6 %collective-permute-start.23 = (bf16[2,128,1024]{2,1,0:T(8,128)(2,1)S(1)}, bf16[2,128,1024]{2,1,0:T(8,128)(2,1)S(1)}, u32[]{:S(2)}, u32[]{:S(2)}) collective-permute-start(bf16[2,128,1024]{2,1,0:T(8,128)(2,1)S(1)} %dynamic-slice_bitcast_fusion.3), channel_id=1, source_target_pairs={{0,2},{1,3},{2,0},{3,1},{4,6},{5,7},{6,4},{7,5},{8,10},{9,11},{10,... | collective-permute-start | bytes 1572872 | tf_op jit(solution)/shard_map/ppermute | solution.py:228
  214.1 7.2 %collective-permute-start.26 = (bf16[1,128,1024]{2,1,0:T(8,128)(2,1)S(1)}, bf16[1,128,1024]{2,1,0:T(8,128)(2,1)S(1)}, u32[]{:S(2)}, u32[]{:S(2)}) collective-permute-start(bf16[1,128,1024]{2,1,0:T(8,128)(2,1)S(1)} %constant_dynamic-slice_fusion), channel_id=1, source_target_pairs={{0,2},{1,3},{2,0},{3,1},{4,6},{5,7},{6,4},{7,5},{8,10},{9,11},{10,... | collective-permute-start | bytes 786440 | tf_op jit(solution)/shard_map/ppermute | solution.py:228
  217.1 7.6 %copy-start.1 = (bf16[512,2048]{1,0:T(8,128)(2,1)S(1)}, bf16[512,2048]{1,0:T(8,128)(2,1)}, u32[]{:S(2)}) copy-start(bf16[512,2048]{1,0:T(8,128)(2,1)} %param.28) | copy-start | bytes 6291460
  217.1 6.4 %collective-permute-start.24 = (bf16[1,128,1024]{2,1,0:T(8,128)(2,1)S(1)}, bf16[1,128,1024]{2,1,0:T(8,128)(2,1)S(1)}, u32[]{:S(2)}, u32[]{:S(2)}) collective-permute-start(bf16[1,128,1024]{2,1,0:T(8,128)(2,1)S(1)} %constant_dynamic-slice_fusion.1), channel_id=1, source_target_pairs={{0,4},{1,5},{2,6},{3,7},{4,0},{5,1},{6,2},{7,3},{8,12},{9,13},{10,... | collective-permute-start | bytes 786440 | tf_op jit(solution)/shard_map/ppermute | solution.py:228
Sparse Core Ops, SparseCore 0:
  9.9 45.7 all-gather.2

commit v3 on v2

--- a/solution.py
+++ b/solution.py
@@ -333,7 +333,7 @@
     crossed = [swap(block, devices, bit) for block in blocks]
     needed = [[] for _ in range(calls - 1)]
     for r in range(1, owners):
-        arrival = min((r - 1) * (calls - 1) // (owners - 1), calls - 2)
+        arrival = min((r - 1) * (calls - 1) // (owners - 1) + 1, calls - 2)
         needed[arrival].append(blocks[r])
         if arrival + 1 < calls - 1:
             needed[arrival + 1].append(crossed[r])

time: 235 us -> 232 us (0.987)
  the two profiles are of different devices: /device:TPU:0 before, /device:TPU:8 now
where the time goes in v3:
time: 232 us; the launch traced here: 229 us
  Pallas kernels  65.8 us (28%)
  waiting for transfers between devices  61.6 us (27%)
  starting transfers between devices  26.2 us (11%)
  between operations  22.6 us (10%)
  other arithmetic  20.7 us (9%)
  local copies, waits for them, and re-layouts  18.8 us (8%)
  matrix products  13.4 us (6%)
    ppermute x27, waiting for transfers between devices, swap(): return lax.ppermute(x, axis, [(h, h ^ bit) for h in range(devices)])  61.5 us
    pallas_call x4, Pallas kernels, delta_part(): pl.pallas_call(functools.partial(delta_kernel, len(unread)), grid_spec=pl...  45.6 us
    ppermute x27, starting transfers between devices, swap(): return lax.ppermute(x, axis, [(h, h ^ bit) for h in range(devices)])  26.2 us
    pallas_call x2, Pallas kernels, attend(): pl.pallas_call(functools.partial(attend_kernel, chunk, block_rows, device...  20.2 us
    dot_general x6, matrix products, product(): out = jnp.dot(x.reshape(-1, x.shape[2]), weight, preferred_element_type=f32)  13.1 us
    unnamed x53, local copies, waits for them, and re-layouts  9.1 us
    convert_element_type x9, other arithmetic, add(): return (a.astype(f32) + b.astype(f32)).astype(bf16)  7.38 us
  transfers between devices with their start and end apart: 28, of which 17 were waited for; matrix products, arithmetic and copies ran while one was open for 16% of the time, Pallas kernels for 24%

profile of v3, /device:TPU:8, one launch (start us, length us, event | category | flops | bytes accessed | tf_op | source)
XLA Modules:
  0.0 229.1 jit_solution(5756100864478736764)
XLA Ops:
  7.2 2.0 copy.76
  9.3 0.7 fusion.24
  10.0 0.7 and_select_fusion
  16.5 1.3 convert_element_type.195
  20.4 0.8 constant_dynamic-slice_fusion.17
  21.2 1.6 collective-permute-start.2
  22.7 1.0 collective-permute-start.1
  23.8 1.5 collective-permute-start
  25.2 1.9 constant_dynamic-slice_fusion.12
  27.2 0.9 copy.74
  28.1 1.5 collective-permute-start.3
  30.0 1.3 copy.55
  32.1 1.2 collective-permute-done.2
  33.3 1.0 collective-permute-done.1
  34.4 1.9 pad_maximum_fusion.3.start_ref
  36.3 11.7 %delta_part.4 = (bf16[4,512,512]{2,1,0:T(8,128)(2,1)}, f32[2,4,128,128]{3,2,1,0:T(8,128)}) custom-call(s32[2]{0:T(128)} %get-tuple-element.41.source, bf16[4,512,256]{2,1,0:T(8,128)(2,1)} %q_ref.7, bf16[4,512,256]{2,1,0:T(8,128)(2,1)} %k_ref.7, bf16[4,512,512]{2,1,0:T(8,128)(2,1)} %v_ref.7, bf16[4,512,512]{2,1,0:T(8,128)(2,1)} %gate_ref.7, ...), custom_call_target="tpu_custom_call" | custom-call | flops 10000000000 | bytes 3000000 | tf_op jit(solution)/shard_map/delta_part/pallas_call | solution.py:112
  48.0 1.6 collective-permute-done.3
  49.7 2.0 fusion.15
  51.7 1.1 collective-permute-start.4
  52.8 1.2 collective-permute-start.5
  54.5 11.3 %delta_part.5 = (bf16[4,512,512]{2,1,0:T(8,128)(2,1)}, f32[2,4,128,128]{3,2,1,0:T(8,128)}) custom-call(s32[2]{0:T(128)} %iota.35.source, bf16[4,512,256]{2,1,0:T(8,128)(2,1)} %q_ref.7, bf16[4,512,256]{2,1,0:T(8,128)(2,1)} %k_ref.7, bf16[4,512,512]{2,1,0:T(8,128)(2,1)} %v_ref.7, bf16[4,512,512]{2,1,0:T(8,128)(2,1)} %gate_ref.7, ...), custom_call_target="tpu_custom_call", output_to_operand_aliasing={{0}: (8, {})} | custom-call | flops 10000000000 | bytes 3000000 | tf_op jit(solution)/shard_map/delta_part/pallas_call | solution.py:112
  65.8 2.5 %collective-permute-start.7 = (bf16[1,2,2,128,256]{4,3,2,1,0:T(8,128)(2,1)}, bf16[1,2,2,128,256]{4,3,2,1,0:T(8,128)(2,1)S(1)}, u32[]{:S(2)}, u32[]{:S(2)}) collective-permute-start(bf16[1,2,2,128,256]{4,3,2,1,0:T(8,128)(2,1)} %get-tuple-element.34), channel_id=1, source_target_pairs={{0,16},{8,24},{16,0},{24,8},{1,17},{9,25},{17,1},{25,9},{2,18},{10... | collective-permute-start | bytes 786440 | tf_op jit(solution)/shard_map/ppermute | solution.py:228
  70.2 11.2 %delta_part.6 = (bf16[4,512,512]{2,1,0:T(8,128)(2,1)}, f32[2,4,128,128]{3,2,1,0:T(8,128)}) custom-call(s32[2]{0:T(128)} %get-tuple-element.42.source, bf16[4,512,256]{2,1,0:T(8,128)(2,1)} %q_ref.7, bf16[4,512,256]{2,1,0:T(8,128)(2,1)} %k_ref.7, bf16[4,512,512]{2,1,0:T(8,128)(2,1)} %v_ref.7, ...), custom_call_target="tpu_custom_call", output_to_operand_aliasing={{0}: (8, {})} | custom-call | flops 10000000000 | bytes 3000000 | tf_op jit(solution)/shard_map/delta_part/pallas_call | solution.py:112
  81.4 2.6 %collective-permute-done.7.refs_2_ = bf16[1,2,2,128,256]{4,3,2,1,0:T(8,128)(2,1)S(1)} collective-permute-done((bf16[1,2,2,128,256]{4,3,2,1,0:T(8,128)(2,1)}, bf16[1,2,2,128,256]{4,3,2,1,0:T(8,128)(2,1)S(1)}, u32[]{:S(2)}, u32[]{:S(2)}) %collective-permute-start.7) | collective-permute-done | bytes 262176 | tf_op jit(solution)/shard_map/ppermute | solution.py:228
  84.0 5.2 %collective-permute-done.8.refs_3_ = bf16[1,2,2,128,256]{4,3,2,1,0:T(8,128)(2,1)S(1)} collective-permute-done((bf16[1,2,2,128,256]{4,3,2,1,0:T(8,128)(2,1)S(1)}, bf16[1,2,2,128,256]{4,3,2,1,0:T(8,128)(2,1)S(1)}, u32[]{:S(2)}, u32[]{:S(2)}) %collective-permute-start.8) | collective-permute-done | bytes 262176 | tf_op jit(solution)/shard_map/ppermute | solution.py:228
  90.1 11.4 %delta_part.7 = (bf16[4,512,512]{2,1,0:T(8,128)(2,1)}, f32[2,4,128,128]{3,2,1,0:T(8,128)}) custom-call(s32[2]{0:T(128)} %iota.30.source, bf16[4,512,256]{2,1,0:T(8,128)(2,1)} %q_ref.7, bf16[4,512,256]{2,1,0:T(8,128)(2,1)} %k_ref.7, bf16[4,512,512]{2,1,0:T(8,128)(2,1)} %v_ref.7, bf16[4,512,512]{2,1,0:T(8,128)(2,1)} %gate_ref.7, ...), custom_call_target="tpu_custom_call", output_to_operand_aliasing={{0}: (8, {})} | custom-call | flops 10000000000 | bytes 3000000 | tf_op jit(solution)/shard_map/delta_part/pallas_call | solution.py:112
  101.5 1.7 constant_dynamic-slice_fusion.10
  103.2 4.3 %convolution_convert_fusion = bf16[1024,2048]{1,0:T(8,128)(2,1)} fusion(bf16[1024,512]{1,0:T(8,128)(2,1)S(1)} %bitcast.142, bf16[512,2048]{1,0:T(8,128)(2,1)S(1)} %copy-done), kind=kOutput, calls=%fused_computation.6 | convolution fusion | flops 2149580800 | bytes 7340032 | tf_op jit(solution)/shard_map/dot_general | solution.py:247
  108.1 1.5 collective-permute-start.14
  109.6 7.1 %collective-permute-done.15 = bf16[1,2,2,128,256]{4,3,2,1,0:T(8,128)(2,1)S(1)} collective-permute-done((bf16[1,2,2,128,256]{4,3,2,1,0:T(8,128)(2,1)S(1)}, bf16[1,2,2,128,256]{4,3,2,1,0:T(8,128)(2,1)S(1)}, u32[]{:S(2)}, u32[]{:S(2)}) %collective-permute-start.15) | collective-permute-done | bytes 262176 | tf_op jit(solution)/shard_map/ppermute | solution.py:228
  116.7 5.2 %collective-permute-done.14 = bf16[1,2,2,128,256]{4,3,2,1,0:T(8,128)(2,1)S(1)} collective-permute-done((bf16[1,2,2,128,256]{4,3,2,1,0:T(8,128)(2,1)S(1)}, bf16[1,2,2,128,256]{4,3,2,1,0:T(8,128)(2,1)S(1)}, u32[]{:S(2)}, u32[]{:S(2)}) %collective-permute-start.14) | collective-permute-done | bytes 262176 | tf_op jit(solution)/shard_map/ppermute | solution.py:228
  121.9 1.4 maximum_maximum_fusion.near_ref
  123.5 2.3 pad_maximum_fusion.2
  125.8 2.4 %convolution_convert_fusion.1 = bf16[1024,2048]{1,0:T(8,128)(2,1)S(1)} fusion(bf16[1024,512]{1,0:T(8,128)(2,1)S(1)} %bitcast.141, bf16[512,2048]{1,0:T(8,128)(2,1)S(1)} %copy-done), kind=kOutput, calls=%fused_computation.7 | convolution fusion | flops 2149580800 | bytes 7340032 | tf_op jit(solution)/shard_map/dot_general | solution.py:247
  128.1 4.1 %fusion.refs_0_ = bf16[4,256,2048]{2,1,0:T(8,128)(2,1)S(1)} fusion(bf16[4,256,2048]{2,1,0:T(8,128)(2,1)S(1)} %bitcast.127, bf16[4,256,2048]{2,1,0:T(8,128)(2,1)} %collective-permute-done.9), kind=kLoop, calls=%fused_computation.1 | loop fusion | flops 8388608 | bytes 12582912 | tf_op jit(solution)/shard_map/convert_element_type | solution.py:243
  132.9 1.5 copy-done.4
  134.4 1.6 collective-permute-start.12
  137.3 10.0 %attend.2 = bf16[4,2,128,512]{3,2,1,0:T(8,128)(2,1)S(1)} custom-call(s32[6]{0:T(128)S(1)} %pad_add_fusion.scalars, s32[4]{0:T(128)S(1)} %dynamic_slice.167.lengths, bf16[4,2,256,512]{3,2,1,0:T(8,128)(2,1)S(1)} %bitcast.119, bf16[4,2,256,512]{3,2,1,0:T(8,128)(2,1)S(1)} %bitcast.122, bf16[4,4,2,128,256]{4,3,2,1,0:T(8,128)(2,1)} %maximum_maximum_fusion.near_ref, ...), custom_call_target="tpu_custom_call" | custom-call | flops 10000000000 | bytes 8000000 | tf_op jit(solution)/shard_map/attend/pallas_call | solution.py:203
  147.5 1.5 copy-done.22
  149.0 2.6 %convolution_convert_fusion.4 = bf16[512,2048]{1,0:T(8,128)(2,1)} fusion(bf16[512,512]{1,0:T(8,128)(2,1)S(1)} %bitcast.151, bf16[512,2048]{1,0:T(8,128)(2,1)S(1)} %copy-done.22), kind=kOutput, calls=%fused_computation.10 | convolution fusion | flops 1074790400 | bytes 4718592 | tf_op jit(solution)/shard_map/dot_general | solution.py:247
  152.1 1.3 convolution_convert_fusion.5
  153.4 6.7 %collective-permute-done.12 = bf16[2,256,1024]{2,1,0:T(8,128)(2,1)S(1)} collective-permute-done((bf16[2,256,1024]{2,1,0:T(8,128)(2,1)S(1)}, bf16[2,256,1024]{2,1,0:T(8,128)(2,1)S(1)}, u32[]{:S(2)}, u32[]{:S(2)}) %collective-permute-start.12) | collective-permute-done | bytes 1048608 | tf_op jit(solution)/shard_map/ppermute | solution.py:228
  161.9 1.4 collective-permute-start.11
  163.3 10.2 %attend.3 = bf16[4,2,128,512]{3,2,1,0:T(8,128)(2,1)S(1)} custom-call(s32[6]{0:T(128)S(1)} %pad_add_fusion.scalars, s32[4]{0:T(128)S(1)} %dynamic_slice.167.lengths, bf16[4,2,256,512]{3,2,1,0:T(8,128)(2,1)S(1)} %bitcast.120, bf16[4,2,256,512]{3,2,1,0:T(8,128)(2,1)} %bitcast.121, bf16[4,4,2,128,256]{4,3,2,1,0:T(8,128)(2,1)} %maximum_maximum_fusion.near_ref, ...), custom_call_target="tpu_custom_call" | custom-call | flops 10000000000 | bytes 8000000 | tf_op jit(solution)/shard_map/attend/pallas_call | solution.py:203
  173.5 1.5 copy-done.23
  175.0 1.3 convolution_convert_fusion.2
  176.4 1.3 convolution_convert_fusion.3
  177.9 0.9 fusion.2
  179.0 0.8 collective-permute-start.20
  180.0 1.1 pad_maximum_fusion
  181.1 1.2 collective-permute-start.18
  182.3 11.1 %collective-permute-done.20 = bf16[2,128,1024]{2,1,0:T(8,128)(2,1)S(1)} collective-permute-done((bf16[2,128,1024]{2,1,0:T(8,128)(2,1)S(1)}, bf16[2,128,1024]{2,1,0:T(8,128)(2,1)S(1)}, u32[]{:S(2)}, u32[]{:S(2)}) %collective-permute-start.20) | collective-permute-done | bytes 524320 | tf_op jit(solution)/shard_map/ppermute | solution.py:228
  193.6 1.5 collective-permute-start.21
  195.1 0.8 fusion.1
  197.0 1.6 collective-permute-start.19
  198.6 0.7 collective-permute-start.23
  199.3 3.6 %collective-permute-done.21 = bf16[1,128,1024]{2,1,0:T(8,128)(2,1)S(1)} collective-permute-done((bf16[1,128,1024]{2,1,0:T(8,128)(2,1)S(1)}, bf16[1,128,1024]{2,1,0:T(8,128)(2,1)S(1)}, u32[]{:S(2)}, u32[]{:S(2)}) %collective-permute-start.21) | collective-permute-done | bytes 262176 | tf_op jit(solution)/shard_map/ppermute | solution.py:228
  203.0 8.1 %collective-permute-done.25 = bf16[2,128,1024]{2,1,0:T(8,128)(2,1)S(1)} collective-permute-done((bf16[2,128,1024]{2,1,0:T(8,128)(2,1)S(1)}, bf16[2,128,1024]{2,1,0:T(8,128)(2,1)S(1)}, u32[]{:S(2)}, u32[]{:S(2)}) %collective-permute-start.25) | collective-permute-done | bytes 524320 | tf_op jit(solution)/shard_map/ppermute | solution.py:228
  211.3 0.7 collective-permute-start.26
  212.0 2.1 collective-permute-done.23
  214.4 0.8 collective-permute-start.24
  215.6 2.8 %collective-permute-done.26 = bf16[1,128,1024]{2,1,0:T(8,128)(2,1)S(1)} collective-permute-done((bf16[1,128,1024]{2,1,0:T(8,128)(2,1)S(1)}, bf16[1,128,1024]{2,1,0:T(8,128)(2,1)S(1)}, u32[]{:S(2)}, u32[]{:S(2)}) %collective-permute-start.26) | collective-permute-done | bytes 262176 | tf_op jit(solution)/shard_map/ppermute | solution.py:228
  218.5 2.3 collective-permute-done.24
  220.9 1.1 maximum_maximum_fusion.1
  (116 shorter events, 13.7 us)
Async XLA Ops:
  7.2 96.0 %copy-start = (bf16[512,2048]{1,0:T(8,128)(2,1)S(1)}, bf16[512,2048]{1,0:T(8,128)(2,1)}, u32[]{:S(2)}) copy-start(bf16[512,2048]{1,0:T(8,128)(2,1)} %param.28) | copy-start | bytes 6291460
  7.2 82.1 %all-gather.3.cloned.1.call-start = ((), (), s32[]{:S(2)}) async-start(), calls=%async_computation | async-start | bytes 4718592 | tf_op jit(solution)/shard_map/all_gather | solution.py:323
  20.4 9.3 %copy-start.19 = (f32[4,4,512]{2,1,0:T(4,128)S(1)}, f32[4,4,512]{2,1,0:T(4,128)}, u32[]{:S(2)}) copy-start(f32[4,4,512]{2,1,0:T(4,128)} %param.20) | copy-start | bytes 98308
  20.4 9.6 %copy-start.20 = (f32[4,4,512]{2,1,0:T(4,128)S(1)}, f32[4,4,512]{2,1,0:T(4,128)}, u32[]{:S(2)}) copy-start(f32[4,4,512]{2,1,0:T(4,128)} %param.19) | copy-start | bytes 98308
  21.2 12.1 %collective-permute-start.2 = (bf16[1,4,128,128]{3,2,1,0:T(8,128)(2,1)}, bf16[1,4,128,128]{3,2,1,0:T(8,128)(2,1)}, u32[]{:S(2)}, u32[]{:S(2)}) collective-permute-start(bf16[1,4,128,128]{3,2,1,0:T(8,128)(2,1)} %get-tuple-element.38), channel_id=1, source_target_pairs={{0,24},{8,16},{16,8},{24,0},{1,25},{9,17},{17,9},{25,1},{2,26},{10... | collective-permute-start | bytes 393224 | tf_op jit(solution)/shard_map/ppermute | solution.py:228
  22.7 11.5 %collective-permute-start.1 = (bf16[1,4,128,128]{3,2,1,0:T(8,128)(2,1)}, bf16[1,4,128,128]{3,2,1,0:T(8,128)(2,1)}, u32[]{:S(2)}, u32[]{:S(2)}) collective-permute-start(bf16[1,4,128,128]{3,2,1,0:T(8,128)(2,1)} %get-tuple-element.39), channel_id=1, source_target_pairs={{0,16},{8,24},{16,0},{24,8},{1,17},{9,25},{17,1},{25,9},{2,18},{10... | collective-permute-start | bytes 393224 | tf_op jit(solution)/shard_map/ppermute | solution.py:228
  23.8 10.7 %collective-permute-start = (bf16[1,4,128,128]{3,2,1,0:T(8,128)(2,1)S(1)}, bf16[1,4,128,128]{3,2,1,0:T(8,128)(2,1)}, u32[]{:S(2)}, u32[]{:S(2)}) collective-permute-start(bf16[1,4,128,128]{3,2,1,0:T(8,128)(2,1)S(1)} %get-tuple-element.40), channel_id=1, source_target_pairs={{0,8},{8,0},{16,24},{24,16},{1,9},{9,1},{17,25},{25,17},{2,10},{10... | collective-permute-start | bytes 393224 | tf_op jit(solution)/shard_map/ppermute | solution.py:228
  27.2 4.2 %copy-start.21 = (s32[16]{0:T(128)S(1)}, s32[16]{0:T(128)}, u32[]{:S(2)}) copy-start(s32[16]{0:T(128)} %param.27) | copy-start | bytes 196
  28.1 21.6 %collective-permute-start.3 = (bf16[4,2,128,256]{3,2,1,0:T(8,128)(2,1)}, bf16[4,2,128,256]{3,2,1,0:T(8,128)(2,1)}, u32[]{:S(2)}, u32[]{:S(2)}) collective-permute-start(bf16[4,2,128,256]{3,2,1,0:T(8,128)(2,1)} %bitcast.116), channel_id=1, source_target_pairs={{0,4},{1,5},{2,6},{3,7},{4,0},{5,1},{6,2},{7,3},{8,12},{9,13},{10,... | collective-permute-start | bytes 1572872 | tf_op jit(solution)/shard_map/ppermute | solution.py:228
  29.9 6.4 %copy-start.18 = (f32[4,4,512]{2,1,0:T(4,128)}, f32[4,4,512]{2,1,0:T(4,128)S(1)}, u32[]{:S(2)}) copy-start(f32[4,4,512]{2,1,0:T(4,128)S(1)} %reshape.199.row_ref) | copy-start | bytes 98308
  51.7 17.3 %collective-permute-start.4 = (bf16[1,2,2,128,256]{4,3,2,1,0:T(8,128)(2,1)}, bf16[1,2,2,128,256]{4,3,2,1,0:T(8,128)(2,1)S(1)}, u32[]{:S(2)}, u32[]{:S(2)}) collective-permute-start(bf16[1,2,2,128,256]{4,3,2,1,0:T(8,128)(2,1)} %get-tuple-element.32), channel_id=1, source_target_pairs={{0,8},{8,0},{16,24},{24,16},{1,9},{9,1},{17,25},{25,17},{2,10},{10... | collective-permute-start | bytes 786440 | tf_op jit(solution)/shard_map/ppermute | solution.py:228
  52.8 16.7 %collective-permute-start.5 = (bf16[1,2,2,128,256]{4,3,2,1,0:T(8,128)(2,1)S(1)}, bf16[1,2,2,128,256]{4,3,2,1,0:T(8,128)(2,1)S(1)}, u32[]{:S(2)}, u32[]{:S(2)}) collective-permute-start(bf16[1,2,2,128,256]{4,3,2,1,0:T(8,128)(2,1)S(1)} %get-tuple-element.33), channel_id=1, source_target_pairs={{0,2},{1,3},{2,0},{3,1},{4,6},{5,7},{6,4},{7,5},{8,10},{9,11},{10,... | collective-permute-start | bytes 786440 | tf_op jit(solution)/shard_map/ppermute | solution.py:228
  54.5 13.9 %copy-start.17 = (bf16[1,2,2,128,256]{4,3,2,1,0:T(8,128)(2,1)S(1)}, bf16[1,2,2,128,256]{4,3,2,1,0:T(8,128)(2,1)}, u32[]{:S(2)}) copy-start(bf16[1,2,2,128,256]{4,3,2,1,0:T(8,128)(2,1)} %get-tuple-element.31) | copy-start | bytes 786436
  65.8 18.2 %collective-permute-start.7 = (bf16[1,2,2,128,256]{4,3,2,1,0:T(8,128)(2,1)}, bf16[1,2,2,128,256]{4,3,2,1,0:T(8,128)(2,1)S(1)}, u32[]{:S(2)}, u32[]{:S(2)}) collective-permute-start(bf16[1,2,2,128,256]{4,3,2,1,0:T(8,128)(2,1)} %get-tuple-element.34), channel_id=1, source_target_pairs={{0,16},{8,24},{16,0},{24,8},{1,17},{9,25},{17,1},{25,9},{2,18},{10... | collective-permute-start | bytes 786440 | tf_op jit(solution)/shard_map/ppermute | solution.py:228
  68.4 20.9 %collective-permute-start.8 = (bf16[1,2,2,128,256]{4,3,2,1,0:T(8,128)(2,1)S(1)}, bf16[1,2,2,128,256]{4,3,2,1,0:T(8,128)(2,1)S(1)}, u32[]{:S(2)}, u32[]{:S(2)}) collective-permute-start(bf16[1,2,2,128,256]{4,3,2,1,0:T(8,128)(2,1)S(1)} %copy-done.17), channel_id=1, source_target_pairs={{0,24},{8,16},{16,8},{24,0},{1,25},{9,17},{17,9},{25,1},{2,26},{10... | collective-permute-start | bytes 786440 | tf_op jit(solution)/shard_map/ppermute | solution.py:228
  69.0 0.7 copy-start.7
  69.0 20.2 %collective-permute-start.6 = (bf16[1,2,2,128,256]{4,3,2,1,0:T(8,128)(2,1)S(1)}, bf16[1,2,2,128,256]{4,3,2,1,0:T(8,128)(2,1)S(1)}, u32[]{:S(2)}, u32[]{:S(2)}) collective-permute-start(bf16[1,2,2,128,256]{4,3,2,1,0:T(8,128)(2,1)S(1)} %collective-permute-done.4.refs_1_), channel_id=1, source_target_pairs={{0,2},{1,3},{2,0},{3,1},{4,6},{5,7},{6,4},{7,5},{8,10},{9,11},{10,... | collective-permute-start | bytes 786440 | tf_op jit(solution)/shard_map/ppermute | solution.py:228
  69.5 0.7 copy-start.9
  84.0 5.8 %copy-start.11 = (bf16[1,2,2,128,256]{4,3,2,1,0:T(8,128)(2,1)}, bf16[1,2,2,128,256]{4,3,2,1,0:T(8,128)(2,1)S(1)}, u32[]{:S(2)}) copy-start(bf16[1,2,2,128,256]{4,3,2,1,0:T(8,128)(2,1)S(1)} %collective-permute-done.7.refs_2_) | copy-start | bytes 786436
  89.2 0.7 copy-start.13
  89.3 0.8 copy-start.15
  103.2 4.4 %copy-start.14 = (bf16[1,2,2,128,256]{4,3,2,1,0:T(8,128)(2,1)S(1)}, bf16[1,2,2,128,256]{4,3,2,1,0:T(8,128)(2,1)}, u32[]{:S(2)}) copy-start(bf16[1,2,2,128,256]{4,3,2,1,0:T(8,128)(2,1)} %copy-done.13) | copy-start | bytes 786436
  103.2 5.0 %copy-start.12 = (bf16[1,2,2,128,256]{4,3,2,1,0:T(8,128)(2,1)S(1)}, bf16[1,2,2,128,256]{4,3,2,1,0:T(8,128)(2,1)}, u32[]{:S(2)}) copy-start(bf16[1,2,2,128,256]{4,3,2,1,0:T(8,128)(2,1)} %copy-done.11) | copy-start | bytes 786436
  103.2 18.7 %copy-start.8 = (bf16[1,2,2,128,256]{4,3,2,1,0:T(8,128)(2,1)S(1)}, bf16[1,2,2,128,256]{4,3,2,1,0:T(8,128)(2,1)}, u32[]{:S(2)}) copy-start(bf16[1,2,2,128,256]{4,3,2,1,0:T(8,128)(2,1)} %copy-done.7) | copy-start | bytes 786436
  103.2 18.7 %copy-start.10 = (bf16[1,2,2,128,256]{4,3,2,1,0:T(8,128)(2,1)S(1)}, bf16[1,2,2,128,256]{4,3,2,1,0:T(8,128)(2,1)}, u32[]{:S(2)}) copy-start(bf16[1,2,2,128,256]{4,3,2,1,0:T(8,128)(2,1)} %copy-done.9) | copy-start | bytes 786436
  103.2 18.7 %copy-start.16 = (bf16[1,2,2,128,256]{4,3,2,1,0:T(8,128)(2,1)S(1)}, bf16[1,2,2,128,256]{4,3,2,1,0:T(8,128)(2,1)}, u32[]{:S(2)}) copy-start(bf16[1,2,2,128,256]{4,3,2,1,0:T(8,128)(2,1)} %copy-done.15) | copy-start | bytes 786436
  107.6 20.6 %collective-permute-start.9 = (bf16[4,256,2048]{2,1,0:T(8,128)(2,1)}, bf16[4,256,2048]{2,1,0:T(8,128)(2,1)}, u32[]{:S(2)}, u32[]{:S(2)}) collective-permute-start(bf16[4,256,2048]{2,1,0:T(8,128)(2,1)} %bitcast.16), channel_id=1, source_target_pairs={{0,1},{1,0},{2,3},{3,2},{4,5},{5,4},{6,7},{7,6},{8,9},{9,8},{10,11... | collective-permute-start | bytes 12582920 | tf_op jit(solution)/shard_map/ppermute | solution.py:228
  107.6 9.1 %collective-permute-start.15 = (bf16[1,2,2,128,256]{4,3,2,1,0:T(8,128)(2,1)S(1)}, bf16[1,2,2,128,256]{4,3,2,1,0:T(8,128)(2,1)S(1)}, u32[]{:S(2)}, u32[]{:S(2)}) collective-permute-start(bf16[1,2,2,128,256]{4,3,2,1,0:T(8,128)(2,1)S(1)} %copy-done.14), channel_id=1, source_target_pairs={{0,2},{1,3},{2,0},{3,1},{4,6},{5,7},{6,4},{7,5},{8,10},{9,11},{10,... | collective-permute-start | bytes 786440 | tf_op jit(solution)/shard_map/ppermute | solution.py:228
  108.1 13.8 %collective-permute-start.14 = (bf16[1,2,2,128,256]{4,3,2,1,0:T(8,128)(2,1)S(1)}, bf16[1,2,2,128,256]{4,3,2,1,0:T(8,128)(2,1)S(1)}, u32[]{:S(2)}, u32[]{:S(2)}) collective-permute-start(bf16[1,2,2,128,256]{4,3,2,1,0:T(8,128)(2,1)S(1)} %copy-done.12), channel_id=1, source_target_pairs={{0,2},{1,3},{2,0},{3,1},{4,6},{5,7},{6,4},{7,5},{8,10},{9,11},{10,... | collective-permute-start | bytes 786440 | tf_op jit(solution)/shard_map/ppermute | solution.py:228
  121.9 1.5 copy-start.24
  123.3 13.4 %collective-permute-start.16 = (bf16[4,4,2,128,256]{4,3,2,1,0:T(8,128)(2,1)}, bf16[4,4,2,128,256]{4,3,2,1,0:T(8,128)(2,1)}, u32[]{:S(2)}, u32[]{:S(2)}) collective-permute-start(bf16[4,4,2,128,256]{4,3,2,1,0:T(8,128)(2,1)} %maximum_maximum_fusion.near_ref), channel_id=1, source_target_pairs={{0,1},{1,0},{2,3},{3,2},{4,5},{5,4},{6,7},{7,6},{8,9},{9,8},{10,11... | collective-permute-start | bytes 6291464 | tf_op jit(solution)/shard_map/ppermute | solution.py:228
  132.2 2.1 copy-start.4
  134.3 1.7 copy-start.5
  134.3 2.4 %copy-start.2 = (bf16[4,512,512]{2,1,0:T(8,128)(2,1)S(1)}, bf16[4,512,512]{2,1,0:T(8,128)(2,1)}, u32[]{:S(2)}) copy-start(bf16[4,512,512]{2,1,0:T(8,128)(2,1)} %param.24) | copy-start | bytes 6291460
  134.3 3.0 %copy-start.3 = (bf16[4,512,512]{2,1,0:T(8,128)(2,1)S(1)}, bf16[4,512,512]{2,1,0:T(8,128)(2,1)}, u32[]{:S(2)}) copy-start(bf16[4,512,512]{2,1,0:T(8,128)(2,1)} %param.25) | copy-start | bytes 6291460
  134.4 25.6 %collective-permute-start.12 = (bf16[2,256,1024]{2,1,0:T(8,128)(2,1)S(1)}, bf16[2,256,1024]{2,1,0:T(8,128)(2,1)S(1)}, u32[]{:S(2)}, u32[]{:S(2)}) collective-permute-start(bf16[2,256,1024]{2,1,0:T(8,128)(2,1)S(1)} %dynamic-slice_bitcast_fusion), channel_id=1, source_target_pairs={{0,4},{1,5},{2,6},{3,7},{4,0},{5,1},{6,2},{7,3},{8,12},{9,13},{10,... | collective-permute-start | bytes 3145736 | tf_op jit(solution)/shard_map/ppermute | solution.py:228
  136.1 25.4 %collective-permute-start.10 = (bf16[2,256,1024]{2,1,0:T(8,128)(2,1)S(1)}, bf16[2,256,1024]{2,1,0:T(8,128)(2,1)S(1)}, u32[]{:S(2)}, u32[]{:S(2)}) collective-permute-start(bf16[2,256,1024]{2,1,0:T(8,128)(2,1)S(1)} %dynamic-slice_bitcast_fusion.1), channel_id=1, source_target_pairs={{0,2},{1,3},{2,0},{3,1},{4,6},{5,7},{6,4},{7,5},{8,10},{9,11},{10,... | collective-permute-start | bytes 3145736 | tf_op jit(solution)/shard_map/ppermute | solution.py:228
  147.4 1.6 copy-start.22
  151.6 26.3 %collective-permute-start.17 = (bf16[4,128,2048]{2,1,0:T(8,128)(2,1)}, bf16[4,128,2048]{2,1,0:T(8,128)(2,1)S(1)}, u32[]{:S(2)}, u32[]{:S(2)}) collective-permute-start(bf16[4,128,2048]{2,1,0:T(8,128)(2,1)} %bitcast.43.refs_0_), channel_id=1, source_target_pairs={{0,1},{1,0},{2,3},{3,2},{4,5},{5,4},{6,7},{7,6},{8,9},{9,8},{10,11... | collective-permute-start | bytes 6291464 | tf_op jit(solution)/shard_map/ppermute | solution.py:228
  152.1 8.0 %copy-start.6 = (bf16[4,256,1024]{2,1,0:T(8,128)(2,1)S(1)}, bf16[4,256,1024]{2,1,0:T(8,128)(2,1)}, u32[]{:S(2)}) copy-start(bf16[4,256,1024]{2,1,0:T(8,128)(2,1)} %copy-done.5) | copy-start | bytes 6291460
  160.5 17.1 %collective-permute-start.13 = (bf16[1,256,1024]{2,1,0:T(8,128)(2,1)S(1)}, bf16[1,256,1024]{2,1,0:T(8,128)(2,1)S(1)}, u32[]{:S(2)}, u32[]{:S(2)}) collective-permute-start(bf16[1,256,1024]{2,1,0:T(8,128)(2,1)S(1)} %constant_dynamic-slice_fusion.8), channel_id=1, source_target_pairs={{0,2},{1,3},{2,0},{3,1},{4,6},{5,7},{6,4},{7,5},{8,10},{9,11},{10,... | collective-permute-start | bytes 1572872 | tf_op jit(solution)/shard_map/ppermute | solution.py:228
  161.9 17.9 %collective-permute-start.11 = (bf16[1,256,1024]{2,1,0:T(8,128)(2,1)S(1)}, bf16[1,256,1024]{2,1,0:T(8,128)(2,1)S(1)}, u32[]{:S(2)}, u32[]{:S(2)}) collective-permute-start(bf16[1,256,1024]{2,1,0:T(8,128)(2,1)S(1)} %constant_dynamic-slice_fusion.9), channel_id=1, source_target_pairs={{0,4},{1,5},{2,6},{3,7},{4,0},{5,1},{6,2},{7,3},{8,12},{9,13},{10,... | collective-permute-start | bytes 1572872 | tf_op jit(solution)/shard_map/ppermute | solution.py:228
  173.4 1.6 copy-start.23
  176.3 18.8 %collective-permute-start.22 = (bf16[4,128,2048]{2,1,0:T(8,128)(2,1)S(1)}, bf16[4,128,2048]{2,1,0:T(8,128)(2,1)S(1)}, u32[]{:S(2)}, u32[]{:S(2)}) collective-permute-start(bf16[4,128,2048]{2,1,0:T(8,128)(2,1)S(1)} %bitcast.162), channel_id=1, source_target_pairs={{0,1},{1,0},{2,3},{3,2},{4,5},{5,4},{6,7},{7,6},{8,9},{9,8},{10,11... | collective-permute-start | bytes 6291464 | tf_op jit(solution)/shard_map/ppermute | solution.py:228
  179.0 14.4 %collective-permute-start.20 = (bf16[2,128,1024]{2,1,0:T(8,128)(2,1)S(1)}, bf16[2,128,1024]{2,1,0:T(8,128)(2,1)S(1)}, u32[]{:S(2)}, u32[]{:S(2)}) collective-permute-start(bf16[2,128,1024]{2,1,0:T(8,128)(2,1)S(1)} %dynamic-slice_bitcast_fusion.4), channel_id=1, source_target_pairs={{0,4},{1,5},{2,6},{3,7},{4,0},{5,1},{6,2},{7,3},{8,12},{9,13},{10,... | collective-permute-start | bytes 1572872 | tf_op jit(solution)/shard_map/ppermute | solution.py:228
  181.1 15.6 %collective-permute-start.18 = (bf16[2,128,1024]{2,1,0:T(8,128)(2,1)S(1)}, bf16[2,128,1024]{2,1,0:T(8,128)(2,1)S(1)}, u32[]{:S(2)}, u32[]{:S(2)}) collective-permute-start(bf16[2,128,1024]{2,1,0:T(8,128)(2,1)S(1)} %dynamic-slice_bitcast_fusion.5), channel_id=1, source_target_pairs={{0,2},{1,3},{2,0},{3,1},{4,6},{5,7},{6,4},{7,5},{8,10},{9,11},{10,... | collective-permute-start | bytes 1572872 | tf_op jit(solution)/shard_map/ppermute | solution.py:228
  193.6 9.3 %collective-permute-start.21 = (bf16[1,128,1024]{2,1,0:T(8,128)(2,1)S(1)}, bf16[1,128,1024]{2,1,0:T(8,128)(2,1)S(1)}, u32[]{:S(2)}, u32[]{:S(2)}) collective-permute-start(bf16[1,128,1024]{2,1,0:T(8,128)(2,1)S(1)} %constant_dynamic-slice_fusion.4), channel_id=1, source_target_pairs={{0,2},{1,3},{2,0},{3,1},{4,6},{5,7},{6,4},{7,5},{8,10},{9,11},{10,... | collective-permute-start | bytes 786440 | tf_op jit(solution)/shard_map/ppermute | solution.py:228
  196.2 14.9 %collective-permute-start.25 = (bf16[2,128,1024]{2,1,0:T(8,128)(2,1)S(1)}, bf16[2,128,1024]{2,1,0:T(8,128)(2,1)S(1)}, u32[]{:S(2)}, u32[]{:S(2)}) collective-permute-start(bf16[2,128,1024]{2,1,0:T(8,128)(2,1)S(1)} %dynamic-slice_bitcast_fusion.2), channel_id=1, source_target_pairs={{0,4},{1,5},{2,6},{3,7},{4,0},{5,1},{6,2},{7,3},{8,12},{9,13},{10,... | collective-permute-start | bytes 1572872 | tf_op jit(solution)/shard_map/ppermute | solution.py:228
  197.0 18.6 %collective-permute-start.19 = (bf16[1,128,1024]{2,1,0:T(8,128)(2,1)S(1)}, bf16[1,128,1024]{2,1,0:T(8,128)(2,1)S(1)}, u32[]{:S(2)}, u32[]{:S(2)}) collective-permute-start(bf16[1,128,1024]{2,1,0:T(8,128)(2,1)S(1)} %constant_dynamic-slice_fusion.5), channel_id=1, source_target_pairs={{0,4},{1,5},{2,6},{3,7},{4,0},{5,1},{6,2},{7,3},{8,12},{9,13},{10,... | collective-permute-start | bytes 786440 | tf_op jit(solution)/shard_map/ppermute | solution.py:228
  198.6 15.5 %collective-permute-start.23 = (bf16[2,128,1024]{2,1,0:T(8,128)(2,1)S(1)}, bf16[2,128,1024]{2,1,0:T(8,128)(2,1)S(1)}, u32[]{:S(2)}, u32[]{:S(2)}) collective-permute-start(bf16[2,128,1024]{2,1,0:T(8,128)(2,1)S(1)} %dynamic-slice_bitcast_fusion.3), channel_id=1, source_target_pairs={{0,2},{1,3},{2,0},{3,1},{4,6},{5,7},{6,4},{7,5},{8,10},{9,11},{10,... | collective-permute-start | bytes 1572872 | tf_op jit(solution)/shard_map/ppermute | solution.py:228
  211.3 7.1 %collective-permute-start.26 = (bf16[1,128,1024]{2,1,0:T(8,128)(2,1)S(1)}, bf16[1,128,1024]{2,1,0:T(8,128)(2,1)S(1)}, u32[]{:S(2)}, u32[]{:S(2)}) collective-permute-start(bf16[1,128,1024]{2,1,0:T(8,128)(2,1)S(1)} %constant_dynamic-slice_fusion), channel_id=1, source_target_pairs={{0,2},{1,3},{2,0},{3,1},{4,6},{5,7},{6,4},{7,5},{8,10},{9,11},{10,... | collective-permute-start | bytes 786440 | tf_op jit(solution)/shard_map/ppermute | solution.py:228
  214.3 7.6 %copy-start.1 = (bf16[512,2048]{1,0:T(8,128)(2,1)S(1)}, bf16[512,2048]{1,0:T(8,128)(2,1)}, u32[]{:S(2)}) copy-start(bf16[512,2048]{1,0:T(8,128)(2,1)} %param.28) | copy-start | bytes 6291460
  214.4 6.4 %collective-permute-start.24 = (bf16[1,128,1024]{2,1,0:T(8,128)(2,1)S(1)}, bf16[1,128,1024]{2,1,0:T(8,128)(2,1)S(1)}, u32[]{:S(2)}, u32[]{:S(2)}) collective-permute-start(bf16[1,128,1024]{2,1,0:T(8,128)(2,1)S(1)} %constant_dynamic-slice_fusion.1), channel_id=1, source_target_pairs={{0,4},{1,5},{2,6},{3,7},{4,0},{5,1},{6,2},{7,3},{8,12},{9,13},{10,... | collective-permute-start | bytes 786440 | tf_op jit(solution)/shard_map/ppermute | solution.py:228
Sparse Core Ops, SparseCore 0:
  9.9 44.4 all-gather.2
